TPU v7x, 32 devices: a whole 2x2x4 slice. The times are simulated.
32 devices in a mesh: section: 2 (over x), expert: 4 (over z), hidden: 4 (over y, core).
Axes of the slice: x: 2, y: 2, z: 4, core: 2. Of those that a mesh axis runs over, the one named last changes fastest.
Arguments:
- tokens: bfloat16 [4, 64, 7168], P(None, 'expert', 'hidden'), may hold values from -12 to 12
- gate_up: bfloat16 [2, 7168, 2, 16384], P('section', 'hidden', None, 'expert'), may hold values from -0.0625 to 0.0625
- down_proj: bfloat16 [2, 16384, 7168], P('section', 'expert', 'hidden'), may hold values from -0.1875 to 0.1875
- routes: int32 [2, 4, 64, 2], P('section', None, 'expert'), may hold values from 0 to 15, all different within a row; in each aligned block of 16 rows (0 to 15, 16 to 31, ..., all dimensions but the last counted through in order) at most 3 rows name the same one
- gate_weights: bfloat16 [2, 4, 64, 2], P('section', None, 'expert'), may hold values from 0.099609375 to 0.59765625
Outputs:
- layer_outputs: bfloat16 [2, 4, 64, 7168], P('section', None, 'expert', 'hidden')
Inputs may be any that keep to these rules, and one draw needn't show every extreme that they name: `routes`: in every layer and micro-batch a token names 2 different experts, and the 16 tokens of one device (aligned blocks of 16 rows) name any one expert at most 3 times; some expert is named exactly 3 times in some block.
All inputs are finite; a program needn't handle non-finite values.
Results may differ from a plain program's by a relative error of at most 0.008.
Values may be sent and summed in bfloat16 or wider, within the bound.
No kernel may reach another device: no remote copies, remote signals or barrier semaphores. Data moves between devices by JAX's collectives and lax.ppermute only.
A program may use at most 192 MiB of HBM per device.

v0:
```python
import jax
import jax.numpy as jnp
from jax import lax
from jax.sharding import PartitionSpec as P

D = 7168
FFE = 1024
CAP = 3


EPS = 1e-06


def shifted(value, axis, steps):
    count = lax.axis_size(axis)
    first, last = (max(0, -steps), min(count, count - steps))
    return lax.ppermute(value, axis, [(source, source + steps) for source in range(first, last)])


def on_device(tokens, gate_up, down_proj, routes, gate_weights):
    sections = lax.axis_size("section")
    peers = lax.axis_size("expert")
    splits = lax.axis_size("hidden")
    section_id = lax.axis_index("section")
    micro_count, tok_rows, slice_width = tokens.shape
    units_dev = gate_up.shape[3]
    local_units = min(FFE, units_dev)
    local_count = units_dev // local_units
    slot_rows_count = peers * CAP
    slot_count = peers * local_count
    device_ids = jnp.arange(peers, dtype=jnp.int32)
    local_ids = jnp.arange(local_count, dtype=jnp.int32)
    slot_expert = (device_ids[:, None] * units_dev // FFE + local_ids[None, :]).reshape(slot_count)
    capacity_ids = jnp.arange(CAP, dtype=jnp.int32)
    w_in = gate_up[0].reshape(slice_width, 2, local_count, local_units)
    w_in = w_in.reshape(slice_width, 2, local_count, splits, local_units // splits).transpose(
        2, 0, 3, 1, 4
    )
    w_in = w_in.reshape(local_count, slice_width, 2 * local_units)
    w_out = down_proj[0].reshape(local_count, local_units, slice_width)

    def source_tables(route_rows, gate_rows):
        matches = route_rows[:, :, None] == slot_expert[None, None, :]
        chosen = jnp.sum(matches.astype(jnp.int32), axis=1, dtype=jnp.int32)
        weight_dense = jnp.sum(
            jnp.where(matches, gate_rows.astype(jnp.float32)[:, :, None], jnp.float32(0.0)), axis=1
        )
        rank = jnp.cumsum(chosen, axis=0, dtype=jnp.int32) - chosen
        hits = (rank[None, :, :] == capacity_ids[:, None, None]) & (chosen[None, :, :] == 1)
        hits = (
            jnp.transpose(hits, (2, 0, 1)).reshape(slot_count * CAP, tok_rows).astype(jnp.float32)
        )
        spread_weight = jnp.repeat(weight_dense.T, CAP, axis=0)
        return (hits.astype(jnp.bfloat16), (hits * spread_weight).astype(jnp.bfloat16))

    def expert_outputs(expert_rows):
        projected = jnp.einsum(
            "jrd,jdf->jrf", expert_rows, w_in, preferred_element_type=jnp.float32
        )
        widened = expert_rows.astype(jnp.float32)
        squares = jnp.sum(widened * widened, axis=2)
        spread = jnp.broadcast_to(squares[:, :, None], (local_count, slot_rows_count, splits))
        summed, summed_squares = (
            lax.psum_scatter(projected, "hidden", scatter_dimension=2, tiled=True),
            lax.psum_scatter(spread, "hidden", scatter_dimension=2, tiled=True),
        )
        norm_scale = lax.rsqrt(summed_squares / D + EPS)
        unit_share = local_units // splits
        activated = (
            jax.nn.silu(norm_scale * summed[:, :, :unit_share])
            * (norm_scale * summed[:, :, unit_share:])
        ).astype(jnp.bfloat16)
        return jnp.einsum(
            "jru,jud->jrd",
            lax.all_gather(activated, "hidden", axis=2, tiled=True),
            w_out,
            preferred_element_type=jnp.float32,
        ).astype(jnp.bfloat16)

    def run_layer(current, safe_index):
        route_rows = lax.dynamic_index_in_dim(routes[0], safe_index, 0, keepdims=False)
        gate_rows = lax.dynamic_index_in_dim(gate_weights[0], safe_index, 0, keepdims=False)
        placement, combiner = source_tables(route_rows, gate_rows)
        sent = jnp.dot(placement, current, preferred_element_type=jnp.float32).astype(jnp.bfloat16)
        received = lax.all_to_all(sent, "expert", split_axis=0, concat_axis=0, tiled=True)
        expert_rows = (
            received.reshape(peers, local_count, CAP, slice_width)
            .transpose(1, 0, 2, 3)
            .reshape(local_count, slot_rows_count, slice_width)
        )
        out_rows = expert_outputs(expert_rows)
        outgoing = (
            out_rows.reshape(local_count, peers, CAP, slice_width)
            .transpose(1, 0, 2, 3)
            .reshape(slot_count * CAP, slice_width)
        )
        returned = lax.all_to_all(outgoing, "expert", split_axis=0, concat_axis=0, tiled=True)
        mixed = lax.dot_general(
            combiner, returned, (((0,), (0,)), ((), ())), preferred_element_type=jnp.float32
        )
        return (current.astype(jnp.float32) + mixed).astype(jnp.bfloat16)

    def tick(step, carried):
        previous, saved = carried
        incoming = shifted(previous, "section", 1)
        batch_index = step - section_id
        valid = (batch_index >= 0) & (batch_index < micro_count)
        safe_index = jnp.clip(batch_index, 0, micro_count - 1)
        fresh = lax.dynamic_index_in_dim(tokens, safe_index, 0, keepdims=False)
        current = jnp.where(section_id == 0, fresh, incoming)
        computed = run_layer(current, safe_index)
        result = jnp.where(valid, computed, current)
        updated = lax.dynamic_update_index_in_dim(saved, result[None], safe_index, 0)
        saved = jnp.where(valid, updated, saved)
        return (result, saved)

    ticks = sections + micro_count - 1
    start_state = jnp.zeros((tok_rows, slice_width), jnp.bfloat16)
    start_saved = jnp.zeros((micro_count, tok_rows, slice_width), jnp.bfloat16)
    _, saved = lax.fori_loop(0, ticks, tick, (start_state, start_saved))
    return saved[None]


def solution(mesh):
    placed = (
        P(None, "expert", "hidden"),
        P("section", "hidden", None, "expert"),
        P("section", "expert", "hidden"),
        P("section", None, "expert", None),
        P("section", None, "expert", None),
    )
    return jax.shard_map(
        on_device,
        mesh=mesh,
        in_specs=placed,
        out_specs=P("section", None, "expert", "hidden"),
        check_vma=False,
    )
```

profile of v0, /device:TPU:2, one launch (start us, length us, event | category | flops | bytes accessed | tf_op | source)
XLA Modules:
  0.0 543.5 jit_solution(1591336673228741019)
XLA Ops:
  6.5 48.0 %reshape_reshape_squeeze.3 = bf16[1792,2,4,4,256]{4,3,2,1,0:T(4,128)(2,1)} reshape(bf16[1,1792,2,4096]{3,2,1,0:T(2,128)(2,1)} %param.8) | data formatting | bytes 58720256 | tf_op jit(solution)/shard_map/reshape;reshape;squeeze | solution.py:36
  54.5 49.5 %copy.49 = bf16[1792,2,4,4,256]{4,1,3,0,2:T(2,128)(2,1)} copy(bf16[1792,2,4,4,256]{4,3,2,1,0:T(4,128)(2,1)} %reshape_reshape_squeeze.3) | data formatting | bytes 58720256 | tf_op jit(solution)/shard_map/reshape;reshape;squeeze | solution.py:36
  104.0 47.7 %reshape.183 = bf16[4,1792,2048]{2,1,0:T(8,128)(2,1)} reshape(bf16[4,1792,4,2,256]{4,3,2,1,0:T(2,128)(2,1)} %bitcast.81) | data formatting | bytes 58720256 | tf_op jit(solution)/shard_map/reshape | solution.py:39
  151.7 384.6 %while.18 = (s32[]{:T(128)}, bf16[16,1792]{1,0:T(8,128)(2,1)S(1)}, bf16[4,16,1792]{2,1,0:T(8,128)(2,1)S(1)}, s32[]{:T(128)}, pred[]{:T(512)}, /*index=5*/bf16[4,...) while((s32[]{:T(128)}, bf16[16,1792]{1,0:T(8,128)(2,1)S(1)}, ...), condition=%wide.region_7.8_spmd.clone.clone, body=%wide.region_0.7_spmd.clone.clone.sunk | while | flops 534757664 | bytes 51486744 | solution.py:120
  158.2 11.7 %all_to_all.44 = bf16[4,12,1792]{2,1,0:T(8,128)(2,1)S(1)} all-to-all(bf16[4,12,1792]{2,1,0:T(8,128)(2,1)S(1)} %all_to_all.38), channel_id=1, replica_groups=mesh['section'=2,'expert'=4,'hidden'=4] {'expert'}, dimensions={0} | all-to-all | bytes 344064 | tf_op jit(solution)/shard_map/while/body/eval_jaxpr/all_to_all | solution.py:85
  170.1 12.2 %fusion.51 = f32[4,12,2048]{2,1,0:T(8,128)} fusion(bf16[4,1792,2048]{2,1,0:T(8,128)(2,1)} %get-tuple-element.448, bf16[4,12,1792]{2,0,1:T(4,128)(2,1)S(1)} %bitcast.80), kind=kOutput, calls=%fused_computation.5.clone.1 | convolution fusion | flops 352321536 | bytes 29925376 | tf_op jit(solution)/shard_map/while/body/eval_jaxpr/jrd,jdf->jrf/dot_general | solution.py:57
  190.4 12.8 %reduce-scatter.2.cloned.1.call-done = f32[4,12,512]{2,1,0:T(8,128)} async-done(((f32[4,12,2048]{2,1,0:T(8,128)}), f32[4,12,512]{2,1,0:T(8,128)}) %reduce-scatter.2.cloned.1.call-update) | async-done | bytes 98320 | tf_op jit(solution)/shard_map/while/body/eval_jaxpr/reduce_scatter | solution.py:64
  222.5 8.4 %all-to-all-done.1 = bf16[4,12,1792]{2,1,0:T(8,128)(2,1)S(1)} async-done(((bf16[4,12,1792]{2,1,0:T(8,128)(2,1)}), bf16[4,12,1792]{2,1,0:T(8,128)(2,1)S(1)}, u32[]{:S(2)}, u32[]{:S(2)}) %all-to-all-start.1) | async-done | bytes 172064 | tf_op jit(solution)/shard_map/while/body/eval_jaxpr/all_to_all | solution.py:97
  237.7 9.4 %all_to_all.44 = bf16[4,12,1792]{2,1,0:T(8,128)(2,1)S(1)} all-to-all(bf16[4,12,1792]{2,1,0:T(8,128)(2,1)S(1)} %all_to_all.38), channel_id=1, replica_groups=mesh['section'=2,'expert'=4,'hidden'=4] {'expert'}, dimensions={0} | all-to-all | bytes 344064 | tf_op jit(solution)/shard_map/while/body/eval_jaxpr/all_to_all | solution.py:85
  247.2 12.2 %fusion.51 = f32[4,12,2048]{2,1,0:T(8,128)} fusion(bf16[4,1792,2048]{2,1,0:T(8,128)(2,1)} %get-tuple-element.448, bf16[4,12,1792]{2,0,1:T(4,128)(2,1)S(1)} %bitcast.80), kind=kOutput, calls=%fused_computation.5.clone.1 | convolution fusion | flops 352321536 | bytes 29925376 | tf_op jit(solution)/shard_map/while/body/eval_jaxpr/jrd,jdf->jrf/dot_general | solution.py:57
  267.8 11.6 %reduce-scatter.2.cloned.1.call-done = f32[4,12,512]{2,1,0:T(8,128)} async-done(((f32[4,12,2048]{2,1,0:T(8,128)}), f32[4,12,512]{2,1,0:T(8,128)}) %reduce-scatter.2.cloned.1.call-update) | async-done | bytes 98320 | tf_op jit(solution)/shard_map/while/body/eval_jaxpr/reduce_scatter | solution.py:64
  298.8 8.4 %all-to-all-done.1 = bf16[4,12,1792]{2,1,0:T(8,128)(2,1)S(1)} async-done(((bf16[4,12,1792]{2,1,0:T(8,128)(2,1)}), bf16[4,12,1792]{2,1,0:T(8,128)(2,1)S(1)}, u32[]{:S(2)}, u32[]{:S(2)}) %all-to-all-start.1) | async-done | bytes 172064 | tf_op jit(solution)/shard_map/while/body/eval_jaxpr/all_to_all | solution.py:97
  313.9 9.4 %all_to_all.44 = bf16[4,12,1792]{2,1,0:T(8,128)(2,1)S(1)} all-to-all(bf16[4,12,1792]{2,1,0:T(8,128)(2,1)S(1)} %all_to_all.38), channel_id=1, replica_groups=mesh['section'=2,'expert'=4,'hidden'=4] {'expert'}, dimensions={0} | all-to-all | bytes 344064 | tf_op jit(solution)/shard_map/while/body/eval_jaxpr/all_to_all | solution.py:85
  323.5 12.2 %fusion.51 = f32[4,12,2048]{2,1,0:T(8,128)} fusion(bf16[4,1792,2048]{2,1,0:T(8,128)(2,1)} %get-tuple-element.448, bf16[4,12,1792]{2,0,1:T(4,128)(2,1)S(1)} %bitcast.80), kind=kOutput, calls=%fused_computation.5.clone.1 | convolution fusion | flops 352321536 | bytes 29925376 | tf_op jit(solution)/shard_map/while/body/eval_jaxpr/jrd,jdf->jrf/dot_general | solution.py:57
  344.1 11.6 %reduce-scatter.2.cloned.1.call-done = f32[4,12,512]{2,1,0:T(8,128)} async-done(((f32[4,12,2048]{2,1,0:T(8,128)}), f32[4,12,512]{2,1,0:T(8,128)}) %reduce-scatter.2.cloned.1.call-update) | async-done | bytes 98320 | tf_op jit(solution)/shard_map/while/body/eval_jaxpr/reduce_scatter | solution.py:64
  375.1 8.4 %all-to-all-done.1 = bf16[4,12,1792]{2,1,0:T(8,128)(2,1)S(1)} async-done(((bf16[4,12,1792]{2,1,0:T(8,128)(2,1)}), bf16[4,12,1792]{2,1,0:T(8,128)(2,1)S(1)}, u32[]{:S(2)}, u32[]{:S(2)}) %all-to-all-start.1) | async-done | bytes 172064 | tf_op jit(solution)/shard_map/while/body/eval_jaxpr/all_to_all | solution.py:97
  390.2 9.4 %all_to_all.44 = bf16[4,12,1792]{2,1,0:T(8,128)(2,1)S(1)} all-to-all(bf16[4,12,1792]{2,1,0:T(8,128)(2,1)S(1)} %all_to_all.38), channel_id=1, replica_groups=mesh['section'=2,'expert'=4,'hidden'=4] {'expert'}, dimensions={0} | all-to-all | bytes 344064 | tf_op jit(solution)/shard_map/while/body/eval_jaxpr/all_to_all | solution.py:85
  399.8 12.2 %fusion.51 = f32[4,12,2048]{2,1,0:T(8,128)} fusion(bf16[4,1792,2048]{2,1,0:T(8,128)(2,1)} %get-tuple-element.448, bf16[4,12,1792]{2,0,1:T(4,128)(2,1)S(1)} %bitcast.80), kind=kOutput, calls=%fused_computation.5.clone.1 | convolution fusion | flops 352321536 | bytes 29925376 | tf_op jit(solution)/shard_map/while/body/eval_jaxpr/jrd,jdf->jrf/dot_general | solution.py:57
  420.4 11.6 %reduce-scatter.2.cloned.1.call-done = f32[4,12,512]{2,1,0:T(8,128)} async-done(((f32[4,12,2048]{2,1,0:T(8,128)}), f32[4,12,512]{2,1,0:T(8,128)}) %reduce-scatter.2.cloned.1.call-update) | async-done | bytes 98320 | tf_op jit(solution)/shard_map/while/body/eval_jaxpr/reduce_scatter | solution.py:64
  451.3 8.4 %all-to-all-done.1 = bf16[4,12,1792]{2,1,0:T(8,128)(2,1)S(1)} async-done(((bf16[4,12,1792]{2,1,0:T(8,128)(2,1)}), bf16[4,12,1792]{2,1,0:T(8,128)(2,1)S(1)}, u32[]{:S(2)}, u32[]{:S(2)}) %all-to-all-start.1) | async-done | bytes 172064 | tf_op jit(solution)/shard_map/while/body/eval_jaxpr/all_to_all | solution.py:97
  466.5 9.4 %all_to_all.44 = bf16[4,12,1792]{2,1,0:T(8,128)(2,1)S(1)} all-to-all(bf16[4,12,1792]{2,1,0:T(8,128)(2,1)S(1)} %all_to_all.38), channel_id=1, replica_groups=mesh['section'=2,'expert'=4,'hidden'=4] {'expert'}, dimensions={0} | all-to-all | bytes 344064 | tf_op jit(solution)/shard_map/while/body/eval_jaxpr/all_to_all | solution.py:85
  476.1 12.2 %fusion.51 = f32[4,12,2048]{2,1,0:T(8,128)} fusion(bf16[4,1792,2048]{2,1,0:T(8,128)(2,1)} %get-tuple-element.448, bf16[4,12,1792]{2,0,1:T(4,128)(2,1)S(1)} %bitcast.80), kind=kOutput, calls=%fused_computation.5.clone.1 | convolution fusion | flops 352321536 | bytes 29925376 | tf_op jit(solution)/shard_map/while/body/eval_jaxpr/jrd,jdf->jrf/dot_general | solution.py:57
  496.7 11.6 %reduce-scatter.2.cloned.1.call-done = f32[4,12,512]{2,1,0:T(8,128)} async-done(((f32[4,12,2048]{2,1,0:T(8,128)}), f32[4,12,512]{2,1,0:T(8,128)}) %reduce-scatter.2.cloned.1.call-update) | async-done | bytes 98320 | tf_op jit(solution)/shard_map/while/body/eval_jaxpr/reduce_scatter | solution.py:64
  527.6 8.4 %all-to-all-done.1 = bf16[4,12,1792]{2,1,0:T(8,128)(2,1)S(1)} async-done(((bf16[4,12,1792]{2,1,0:T(8,128)(2,1)}), bf16[4,12,1792]{2,1,0:T(8,128)(2,1)S(1)}, u32[]{:S(2)}, u32[]{:S(2)}) %all-to-all-start.1) | async-done | bytes 172064 | tf_op jit(solution)/shard_map/while/body/eval_jaxpr/all_to_all | solution.py:97
  (234 shorter events, 172.4 us)
Async XLA Ops:
  104.0 47.7 %copy-start = (bf16[4,16,1792]{2,1,0:T(8,128)(2,1)S(1)}, bf16[4,16,1792]{2,1,0:T(8,128)(2,1)}, u32[]{:S(2)}) copy-start(bf16[4,16,1792]{2,1,0:T(8,128)(2,1)} %param.7) | copy-start | bytes 688132
  104.0 47.7 %copy-start.2 = (u32[32]{0:T(128)S(1)}, u32[32]{0:T(128)}, u32[]{:S(2)}) copy-start(u32[32]{0:T(128)} %constant.156) | copy-start | bytes 388
  151.8 51.4 %reduce-scatter.2.cloned.1.call-start = ((), (), s32[]{:S(2)}) async-start(), calls=%async_computation.3 | async-start | bytes 655360 | tf_op jit(solution)/shard_map/while/body/eval_jaxpr/reduce_scatter | solution.py:64
  151.8 6.1 %collective-permute-start = (bf16[16,1792]{1,0:T(8,128)(2,1)S(1)}, bf16[16,1792]{1,0:T(8,128)(2,1)S(1)}, u32[]{:S(2)}, u32[]{:S(2)}) collective-permute-start(bf16[16,1792]{1,0:T(8,128)(2,1)S(1)} %broadcast_select_fusion.2), channel_id=1, source_target_pairs={{0,16},{1,17},{2,18},{3,19},{4,20},{5,21},{6,22},{7,23},{8,24},{9,... | collective-permute-start | bytes 172040 | tf_op jit(solution)/shard_map/while/body/eval_jaxpr/ppermute | solution.py:17
  217.7 13.3 %all-to-all-start.1 = ((bf16[4,12,1792]{2,1,0:T(8,128)(2,1)}), bf16[4,12,1792]{2,1,0:T(8,128)(2,1)S(1)}, u32[]{:S(2)}, u32[]{:S(2)}) async-start(bf16[4,12,1792]{2,1,0:T(8,128)(2,1)} %copy.69), calls=%async_computation.2 | async-start | bytes 458752 | tf_op jit(solution)/shard_map/while/body/eval_jaxpr/all_to_all | solution.py:97
  231.2 48.2 %reduce-scatter.2.cloned.1.call-start = ((), (), s32[]{:S(2)}) async-start(), calls=%async_computation.3 | async-start | bytes 655360 | tf_op jit(solution)/shard_map/while/body/eval_jaxpr/reduce_scatter | solution.py:64
  231.3 6.1 %collective-permute-start = (bf16[16,1792]{1,0:T(8,128)(2,1)S(1)}, bf16[16,1792]{1,0:T(8,128)(2,1)S(1)}, u32[]{:S(2)}, u32[]{:S(2)}) collective-permute-start(bf16[16,1792]{1,0:T(8,128)(2,1)S(1)} %broadcast_select_fusion.2), channel_id=1, source_target_pairs={{0,16},{1,17},{2,18},{3,19},{4,20},{5,21},{6,22},{7,23},{8,24},{9,... | collective-permute-start | bytes 172040 | tf_op jit(solution)/shard_map/while/body/eval_jaxpr/ppermute | solution.py:17
  293.9 13.3 %all-to-all-start.1 = ((bf16[4,12,1792]{2,1,0:T(8,128)(2,1)}), bf16[4,12,1792]{2,1,0:T(8,128)(2,1)S(1)}, u32[]{:S(2)}, u32[]{:S(2)}) async-start(bf16[4,12,1792]{2,1,0:T(8,128)(2,1)} %copy.69), calls=%async_computation.2 | async-start | bytes 458752 | tf_op jit(solution)/shard_map/while/body/eval_jaxpr/all_to_all | solution.py:97
  307.5 48.2 %reduce-scatter.2.cloned.1.call-start = ((), (), s32[]{:S(2)}) async-start(), calls=%async_computation.3 | async-start | bytes 655360 | tf_op jit(solution)/shard_map/while/body/eval_jaxpr/reduce_scatter | solution.py:64
  307.6 6.1 %collective-permute-start = (bf16[16,1792]{1,0:T(8,128)(2,1)S(1)}, bf16[16,1792]{1,0:T(8,128)(2,1)S(1)}, u32[]{:S(2)}, u32[]{:S(2)}) collective-permute-start(bf16[16,1792]{1,0:T(8,128)(2,1)S(1)} %broadcast_select_fusion.2), channel_id=1, source_target_pairs={{0,16},{1,17},{2,18},{3,19},{4,20},{5,21},{6,22},{7,23},{8,24},{9,... | collective-permute-start | bytes 172040 | tf_op jit(solution)/shard_map/while/body/eval_jaxpr/ppermute | solution.py:17
  370.2 13.3 %all-to-all-start.1 = ((bf16[4,12,1792]{2,1,0:T(8,128)(2,1)}), bf16[4,12,1792]{2,1,0:T(8,128)(2,1)S(1)}, u32[]{:S(2)}, u32[]{:S(2)}) async-start(bf16[4,12,1792]{2,1,0:T(8,128)(2,1)} %copy.69), calls=%async_computation.2 | async-start | bytes 458752 | tf_op jit(solution)/shard_map/while/body/eval_jaxpr/all_to_all | solution.py:97
  383.8 48.2 %reduce-scatter.2.cloned.1.call-start = ((), (), s32[]{:S(2)}) async-start(), calls=%async_computation.3 | async-start | bytes 655360 | tf_op jit(solution)/shard_map/while/body/eval_jaxpr/reduce_scatter | solution.py:64
  383.8 6.1 %collective-permute-start = (bf16[16,1792]{1,0:T(8,128)(2,1)S(1)}, bf16[16,1792]{1,0:T(8,128)(2,1)S(1)}, u32[]{:S(2)}, u32[]{:S(2)}) collective-permute-start(bf16[16,1792]{1,0:T(8,128)(2,1)S(1)} %broadcast_select_fusion.2), channel_id=1, source_target_pairs={{0,16},{1,17},{2,18},{3,19},{4,20},{5,21},{6,22},{7,23},{8,24},{9,... | collective-permute-start | bytes 172040 | tf_op jit(solution)/shard_map/while/body/eval_jaxpr/ppermute | solution.py:17
  446.5 13.3 %all-to-all-start.1 = ((bf16[4,12,1792]{2,1,0:T(8,128)(2,1)}), bf16[4,12,1792]{2,1,0:T(8,128)(2,1)S(1)}, u32[]{:S(2)}, u32[]{:S(2)}) async-start(bf16[4,12,1792]{2,1,0:T(8,128)(2,1)} %copy.69), calls=%async_computation.2 | async-start | bytes 458752 | tf_op jit(solution)/shard_map/while/body/eval_jaxpr/all_to_all | solution.py:97
  460.1 48.2 %reduce-scatter.2.cloned.1.call-start = ((), (), s32[]{:S(2)}) async-start(), calls=%async_computation.3 | async-start | bytes 655360 | tf_op jit(solution)/shard_map/while/body/eval_jaxpr/reduce_scatter | solution.py:64
  460.1 6.1 %collective-permute-start = (bf16[16,1792]{1,0:T(8,128)(2,1)S(1)}, bf16[16,1792]{1,0:T(8,128)(2,1)S(1)}, u32[]{:S(2)}, u32[]{:S(2)}) collective-permute-start(bf16[16,1792]{1,0:T(8,128)(2,1)S(1)} %broadcast_select_fusion.2), channel_id=1, source_target_pairs={{0,16},{1,17},{2,18},{3,19},{4,20},{5,21},{6,22},{7,23},{8,24},{9,... | collective-permute-start | bytes 172040 | tf_op jit(solution)/shard_map/while/body/eval_jaxpr/ppermute | solution.py:17
  522.8 13.3 %all-to-all-start.1 = ((bf16[4,12,1792]{2,1,0:T(8,128)(2,1)}), bf16[4,12,1792]{2,1,0:T(8,128)(2,1)S(1)}, u32[]{:S(2)}, u32[]{:S(2)}) async-start(bf16[4,12,1792]{2,1,0:T(8,128)(2,1)} %copy.69), calls=%async_computation.2 | async-start | bytes 458752 | tf_op jit(solution)/shard_map/while/body/eval_jaxpr/all_to_all | solution.py:97
  536.3 0.7 copy-start.1
Sparse Core Ops, SparseCore 0:
  182.4 20.7 reduce-scatter.1
  259.6 19.8 reduce-scatter.1
  335.9 19.8 reduce-scatter.1
  412.2 19.8 reduce-scatter.1
  488.4 19.8 reduce-scatter.1
where the time goes:
time: 549 us; the launch traced here: 544 us
  local copies, waits for them, and re-layouts  161 us (29%)
  waiting for transfers between devices  119 us (22%)
  blocking collectives  106 us (19%)
  matrix products  99.3 us (18%)
  starting transfers between devices  29.7 us (5%)
  other arithmetic  13.8 us (3%)
  between operations  13.1 us (2%)
    another operation x2, local copies, waits for them, and re-layouts, on_device(): w_in.reshape(slice_width, 2, local_count, splits, local_units // splits)  97.5 us
    dot_general x5, matrix products, expert_outputs(): jnp.einsum('jrd,jdf->jrf', expert_rows, w_in, preferred_element_type=jnp....  61.1 us
    reduce_scatter x5, waiting for transfers between devices, expert_outputs(): lax.psum_scatter(projected, 'hidden', scatter_dimension=2, tiled=True)  59.4 us
    all_to_all x5, blocking collectives, run_layer(): lax.all_to_all(sent, 'expert', split_axis=0, concat_axis=0, tiled=True)  49.4 us
    reshape x1, local copies, waits for them, and re-layouts, on_device(): w_in = w_in.reshape(local_count, slice_width, 2 * local_units)  47.7 us
    all_to_all x5, waiting for transfers between devices, run_layer(): lax.all_to_all(outgoing, 'expert', split_axis=0, concat_axis=0, tiled=True)  42.2 us
    dot_general x5, matrix products, expert_outputs(): jnp.einsum('jru,jud->jrd', lax.all_gather(activated, 'hidden', axis=2, ti...  36 us
    while x5, blocking collectives  29.9 us
  transfers between devices with their start and end apart: 15, of which 15 were waited for; matrix products, arithmetic and copies ran while one was open for 3% of the time, Pallas kernels for 0%

commit v1 on v0

v1 whole, which is shorter than its diff:
```python
import functools

import jax
import jax.numpy as jnp
import numpy as np
from jax import lax
from jax.experimental import pallas as pl
from jax.experimental.pallas import tpu as pltpu
from jax.sharding import PartitionSpec as P

D = 7168
FFE = 1024
CAP = 3
EPS = 1e-06
TILE = 16
SMEM = pl.BlockSpec(memory_space=pltpu.SMEM)
VMEM = pl.BlockSpec(memory_space=pltpu.VMEM)
HBM = pl.BlockSpec(memory_space=pl.ANY)
BF16 = jnp.bfloat16
F32 = jnp.float32


def padded(count, unit=TILE):
    return -(-count // unit) * unit


def dot(a, b):
    return jnp.dot(a, b, preferred_element_type=F32)


def swap(value, axis, step):
    count = lax.axis_size(axis)
    return lax.ppermute(value, axis, [(i, i ^ step) for i in range(count)])


class Sizes:
    def __init__(self, tokens, gate_up, peers, splits):
        self.peers, self.splits = peers, splits
        self.micro, self.tok, self.width = tokens.shape
        self.rows = self.micro * self.tok
        units_dev = gate_up.shape[3]
        self.units_dev = units_dev
        self.units = min(FFE, units_dev)
        self.local = units_dev // self.units
        self.share = self.units // splits
        self.slots = self.micro * CAP
        self.pay = padded(self.local * self.slots)
        self.all_pay = peers * self.pay
        self.pieces = peers if peers <= 8 else 1
        self.piece = self.all_pay // self.pieces
        self.each = padded(peers * self.slots)
        self.all_each = self.local * self.each
        self.lanes = 2 * self.share
        self.square_rows = padded(2 * -(-self.all_each // self.lanes))

    def slot_table(self):
        row = np.arange(self.all_pay)
        step, place = row // self.pay, row % self.pay
        expert, batch, rank = place // self.slots, place // CAP % self.micro, place % CAP
        rank = np.where(place < self.local * self.slots, rank, -1)
        return np.stack([step, expert, batch, rank], axis=1).astype(np.int32)

    def reorder(self):
        matrix = np.zeros((self.all_each, self.all_pay), np.float32)
        for expert in range(self.local):
            for step in range(self.peers):
                for slot in range(self.slots):
                    matrix[
                        expert * self.each + step * self.slots + slot,
                        step * self.pay + expert * self.slots + slot,
                    ] = 1.0
        return matrix


def pack_kernel(z, me_ref, table_ref, routes_ref, gates_ref, rows_ref, *outs):
    table = table_ref[...]
    owner = table[:, 0:1] ^ me_ref[0] if z.pieces > 1 else table[:, 0:1]
    if z.units_dev >= FFE:
        expert = owner * z.local + table[:, 1:2]
    else:
        expert = lax.shift_right_logical(owner, (FFE // z.units_dev).bit_length() - 1)
    batch, rank = table[:, 2:3], table[:, 3:4]
    shape = (z.all_pay, z.rows)
    token = lax.broadcasted_iota(jnp.int32, shape, 1)
    start = batch * z.tok
    same = (token >= start) & (token < start + z.tok)
    first = (routes_ref[0:1, :] == expert) & same
    second = (routes_ref[1:2, :] == expert) & same
    chosen = jnp.where(first | second, F32(1.0), F32(0.0))
    square = (z.rows, z.rows)
    before = lax.broadcasted_iota(jnp.int32, square, 0) < lax.broadcasted_iota(jnp.int32, square, 1)
    before = jnp.where(before, F32(1.0), F32(0.0)).astype(BF16)
    count = dot(chosen.astype(BF16), before)
    hits = jnp.where(count == rank.astype(F32), chosen, F32(0.0))
    weight = jnp.where(first, gates_ref[0:1, :], F32(0.0)) + jnp.where(second, gates_ref[1:2, :], F32(0.0))
    outs[z.pieces][...] = (hits * weight).astype(BF16)
    hits = hits.astype(BF16)
    rows = rows_ref[...]
    for step in range(z.pieces):
        outs[step][...] = dot(hits[step * z.piece:(step + 1) * z.piece], rows).astype(BF16)


def up_kernel(z, parts, h_ref, order_ref, *refs):
    received, weights = refs[:z.pieces], refs[z.pieces]
    outs = refs[z.pieces + 1:z.pieces + 1 + z.splits]
    stacked, spread, held, staged, sems = refs[z.pieces + 1 + z.splits:]
    flat = weights.reshape(2 * z.width, z.units_dev)
    depth = 2 * z.width // parts

    def fetch(expert, part):
        return pltpu.make_async_copy(
            flat.at[pl.ds(part * depth, depth), pl.ds(expert * z.units, z.units)],
            held.at[expert * parts + part],
            sems.at[expert * parts + part],
        )

    for expert in range(z.local):
        for part in range(parts):
            fetch(expert, part).start()
    for step in range(z.pieces):
        stacked[step * z.piece:(step + 1) * z.piece, :] = received[step][...]
    rows = dot(order_ref[...], stacked[...])
    squares = rows * rows
    high = squares.astype(BF16)
    low = (squares - high.astype(F32)).astype(BF16)
    ones = jnp.ones((TILE, z.width), BF16)
    across = (((1,), (1,)), ((), ()))
    sums = lax.dot_general(ones, high, across, preferred_element_type=F32) + lax.dot_general(
        ones, low, across, preferred_element_type=F32
    )
    rows = rows.astype(BF16)
    block = 128
    shape = (block, 2 * block)
    target = lax.broadcasted_iota(jnp.int32, shape, 1) - 2 * lax.broadcasted_iota(jnp.int32, shape, 0)
    for side in range(2):
        placing = jnp.where(target == side, F32(1.0), F32(0.0)).astype(BF16)
        for piece in range(z.width // block):
            low_col = 2 * block * piece
            part, offset = low_col // depth, low_col % depth
            wide = dot(rows[:, piece * block:(piece + 1) * block], placing).astype(BF16)
            for expert in range(z.local):
                spread[
                    expert * parts + part,
                    side * z.each:(side + 1) * z.each,
                    offset:offset + 2 * block,
                ] = wide[expert * z.each:(expert + 1) * z.each]
    sum_high = sums.astype(BF16).astype(F32)
    sum_low = sums - sum_high
    row_id = lax.broadcasted_iota(jnp.int32, (z.square_rows, z.lanes), 0)
    extra = jnp.zeros((z.square_rows, z.lanes), F32)
    for piece in range(-(-z.all_each // z.lanes)):
        begin = piece * z.lanes
        end = min(z.all_each, begin + z.lanes)
        both = []
        for value in (sum_high, sum_low):
            value = value[0:1, begin:end]
            if end - begin < z.lanes:
                value = jnp.concatenate([value, jnp.zeros((1, z.lanes - end + begin), F32)], axis=1)
            both.append(value)
        extra = jnp.where(row_id == 2 * piece, both[0], jnp.where(row_id == 2 * piece + 1, both[1], extra))
    for piece in range(z.splits):
        staged[piece, z.all_each:, :] = extra.astype(BF16)
    for expert in range(z.local):
        total = None
        for part in range(parts):
            fetch(expert, part).wait()
            value = dot(spread[expert * parts + part], held[expert * parts + part])
            total = value if total is None else total + value
        total = total.astype(BF16)
        for piece in range(z.splits):
            columns = slice(piece * z.share, (piece + 1) * z.share)
            here = slice(expert * z.each, (expert + 1) * z.each)
            staged[piece, here, 0:z.share] = total[:z.each, columns]
            staged[piece, here, z.share:2 * z.share] = total[z.each:, columns]
    for step in range(z.splits):
        outs[step][...] = staged[h_ref[0] ^ step]


def act_kernel(z, *refs):
    out = refs[z.splits]
    total = refs[0][...].astype(F32)
    for step in range(1, z.splits):
        total = total + refs[step][...].astype(F32)
    extra = total[z.all_each:, :]
    for piece in range(-(-z.all_each // z.lanes)):
        begin = piece * z.lanes
        end = min(z.all_each, begin + z.lanes)
        shape = (end - begin, end - begin)
        line = (extra[2 * piece:2 * piece + 1, :] + extra[2 * piece + 1:2 * piece + 2, :])[:, :end - begin]
        diagonal = lax.broadcasted_iota(jnp.int32, shape, 0) == lax.broadcasted_iota(jnp.int32, shape, 1)
        sums = jnp.sum(jnp.where(diagonal, line, F32(0.0)), axis=1, keepdims=True)
        scale = lax.rsqrt(sums / D + EPS)
        gate = scale * total[begin:end, :z.share]
        up = scale * total[begin:end, z.share:]
        out[begin:end, :] = (gate / (F32(1.0) + jnp.exp(-gate)) * up).astype(BF16)


def down_kernel(z, h_ref, order_ref, *refs):
    units, weights = refs[:z.splits], refs[z.splits]
    outs = refs[z.splits + 1:z.splits + 1 + z.pieces]
    held, result, sems = refs[z.splits + 1 + z.pieces:]

    def fetch(expert):
        return pltpu.make_async_copy(
            weights.at[0, pl.ds(expert * z.units, z.units), :], held.at[expert], sems.at[expert]
        )

    for expert in range(z.local):
        fetch(expert).start()
    for expert in range(z.local):
        fetch(expert).wait()
        here = slice(expert * z.each, (expert + 1) * z.each)
        total = None
        for step in range(z.splits):
            low = pl.multiple_of((h_ref[0] ^ step) * z.share, z.share)
            value = dot(units[step][here, :], held[expert, pl.ds(low, z.share), :])
            total = value if total is None else total + value
        result[here, :] = total.astype(BF16)
    for step in range(z.pieces):
        rows = order_ref[step * z.piece:(step + 1) * z.piece, :]
        outs[step][...] = dot(rows, result[...]).astype(BF16)


def combine_kernel(z, own_ref, weight_ref, rows_ref, kept_ref, *refs):
    returned, out, stacked = refs[:z.pieces], refs[z.pieces], refs[z.pieces + 1]
    for step in range(z.pieces):
        stacked[step * z.piece:(step + 1) * z.piece, :] = returned[step][...]
    mixed = lax.dot_general(
        weight_ref[...], stacked[...], (((0,), (0,)), ((), ())), preferred_element_type=F32
    )
    value = (rows_ref[...].astype(F32) + mixed).astype(BF16)
    out[...] = jnp.where(own_ref[0] == 1, value, kept_ref[...])


def call(kernel, z, megabytes, outs, in_specs, scratch, *args):
    z = z if isinstance(z, tuple) else (z,)
    results = pl.pallas_call(
        functools.partial(kernel, *z),
        out_shape=outs,
        in_specs=in_specs,
        out_specs=[VMEM] * len(outs),
        scratch_shapes=scratch,
        compiler_params=pltpu.CompilerParams(vmem_limit_bytes=megabytes * 2**20),
    )(*args)
    return list(results)


def on_device(tokens, gate_up, down_proj, routes, gate_weights):
    sections = lax.axis_size("section")
    section_id = lax.axis_index("section")
    z = Sizes(tokens, gate_up, lax.axis_size("expert"), lax.axis_size("hidden"))
    me = lax.axis_index("expert").astype(jnp.int32).reshape(1)
    h = lax.axis_index("hidden").astype(jnp.int32).reshape(1)
    table = jnp.asarray(z.slot_table())
    order = z.reorder()
    back = jnp.asarray(order.T, BF16)
    order = jnp.asarray(order, BF16)
    routes2 = routes[0].transpose(2, 0, 1).reshape(2, z.rows)
    gates2 = gate_weights[0].astype(F32).transpose(2, 0, 1).reshape(2, z.rows)
    parts = 2 if z.width % 256 == 0 else 1
    shape = jax.ShapeDtypeStruct
    pay = shape((z.piece, z.width), BF16)
    partial = shape((z.all_each + z.square_rows, z.lanes), BF16)

    def exchanged(pieces):
        if z.pieces == 1:
            return [lax.all_to_all(pieces[0], "expert", split_axis=0, concat_axis=0, tiled=True)]
        return pieces[:1] + [swap(pieces[step], "expert", step) for step in range(1, z.pieces)]

    def layer(rows, kept, tick):
        *sent, weight = call(
            pack_kernel, z, 6,
            [pay] * z.pieces + [shape((z.all_pay, z.rows), BF16)],
            [SMEM] + [VMEM] * 4, [],
            me, table, routes2, gates2, rows,
        )
        received = exchanged(sent)
        sums = call(
            up_kernel, (z, parts), 40,
            [partial] * z.splits,
            [SMEM, VMEM] + [VMEM] * z.pieces + [HBM],
            [
                pltpu.VMEM((z.all_pay, z.width), BF16),
                pltpu.VMEM((z.local * parts, 2 * z.each, 2 * z.width // parts), BF16),
                pltpu.VMEM((z.local * parts, 2 * z.width // parts, z.units), BF16),
                pltpu.VMEM((z.splits,) + partial.shape, BF16),
                pltpu.SemaphoreType.DMA((z.local * parts,)),
            ],
            h, order, *received, gate_up,
        )
        sums = sums[:1] + [swap(sums[step], "hidden", step) for step in range(1, z.splits)]
        units = call(
            act_kernel, z, 6, [shape((z.all_each, z.share), BF16)], [VMEM] * z.splits, [], *sums
        )[0]
        units = [units] + [swap(units, "hidden", step) for step in range(1, z.splits)]
        outgoing = call(
            down_kernel, z, 22,
            [pay] * z.pieces,
            [SMEM, VMEM] + [VMEM] * z.splits + [HBM],
            [
                pltpu.VMEM((z.local, z.units, z.width), BF16),
                pltpu.VMEM((z.all_each, z.width), BF16),
                pltpu.SemaphoreType.DMA((z.local,)),
            ],
            h, back, *units, down_proj,
        )
        returned = exchanged(outgoing)
        own = (section_id == tick).astype(jnp.int32).reshape(1)
        return call(
            combine_kernel, z, 6,
            [shape((z.rows, z.width), BF16)],
            [SMEM] + [VMEM] * (3 + z.pieces),
            [pltpu.VMEM((z.all_pay, z.width), BF16)],
            own, weight, rows, kept, *returned,
        )[0]

    rows = tokens.reshape(z.rows, z.width)
    kept = rows
    for tick in range(sections):
        if tick:
            rows = lax.ppermute(kept, "section", [(tick - 1, tick)])
        kept = layer(rows, kept, tick)
    return kept.reshape(1, z.micro, z.tok, z.width)


def solution(mesh):
    placed = (
        P(None, "expert", "hidden"),
        P("section", "hidden", None, "expert"),
        P("section", "expert", "hidden"),
        P("section", None, "expert", None),
        P("section", None, "expert", None),
    )
    return jax.shard_map(
        on_device,
        mesh=mesh,
        in_specs=placed,
        out_specs=P("section", None, "expert", "hidden"),
        check_vma=False,
    )
```

time: 549 us -> 164 us (0.30)
  local copies, waits for them, and re-layouts: 161 us -> 9.62 us
  blocking collectives: 106 us -> 0 us
  matrix products: 99.3 us -> 0 us
  Pallas kernels: 0 us -> 36.4 us
  waiting for transfers between devices: 119 us -> 86.3 us
  other arithmetic: 13.8 us -> 0.01 us
  between operations: 13.1 us -> 0.15 us
    dot_general x20 -> x0, matrix products: 99.3 us -> none  [the longest x5 61.1 us: expert_outputs(): jnp.einsum('jrd,jdf->jrf', expert_rows, w_in, preferred_element_type=jnp....]
    another operation x2 -> x0, local copies, waits for them, and re-layouts: 97.5 us -> none  [on_device(): w_in.reshape(slice_width, 2, local_count, splits, local_units // splits)]
    ppermute x5 -> x25, waiting for transfers between devices: 17.3 us -> 86.3 us  [the longest x24 79.9 us: swap(): return lax.ppermute(value, axis, [(i, i ^ step) for i in range(count)])]
    reduce_scatter x5 -> x0, waiting for transfers between devices: 59.4 us -> none  [expert_outputs(): lax.psum_scatter(projected, 'hidden', scatter_dimension=2, tiled=True)]
    all_to_all x5 -> x0, blocking collectives: 49.4 us -> none  [run_layer(): lax.all_to_all(sent, 'expert', split_axis=0, concat_axis=0, tiled=True)]
    reshape x1 -> x3, local copies, waits for them, and re-layouts: 47.7 us -> 0.86 us  [the longest x2 0.77 us: on_device(): gates2 = gate_weights[0].astype(F32).transpose(2, 0, 1).reshape(2, z.rows)]
    all_to_all x5 -> x0, waiting for transfers between devices: 42.2 us -> none  [run_layer(): lax.all_to_all(outgoing, 'expert', split_axis=0, concat_axis=0, tiled=True)]
    pallas_call x0 -> x10, Pallas kernels: none -> 36.4 us  [call(): pl.pallas_call(functools.partial(kernel, *z), out_shape=outs, in_specs=in...]
  transfers between devices with their start and end apart: 15 -> 25, of which waited for: 15 -> 17; matrix products, arithmetic and copies ran while one was open for 3% -> 0% of each run, Pallas kernels for 0% -> 0%
where the time goes in v1:
time: 164 us; the launch traced here: 162 us
  waiting for transfers between devices  86.3 us (53%)
  Pallas kernels  36.4 us (22%)
  starting transfers between devices  30 us (18%)
  local copies, waits for them, and re-layouts  9.62 us (6%)
    ppermute x24, waiting for transfers between devices, swap(): return lax.ppermute(value, axis, [(i, i ^ step) for i in range(count)])  79.9 us
    pallas_call x10, Pallas kernels, call(): pl.pallas_call(functools.partial(kernel, *z), out_shape=outs, in_specs=in...  36.4 us
    ppermute x24, starting transfers between devices, swap(): return lax.ppermute(value, axis, [(i, i ^ step) for i in range(count)])  28.5 us
    unnamed x23, local copies, waits for them, and re-layouts  8.77 us
    ppermute x1, waiting for transfers between devices, on_device(): rows = lax.ppermute(kept, 'section', [(tick - 1, tick)])  6.43 us
  transfers between devices with their start and end apart: 25, of which 17 were waited for; matrix products, arithmetic and copies ran while one was open for 0% of the time, Pallas kernels for 0%

profile of v1, /device:TPU:2, one launch (start us, length us, event | category | flops | bytes accessed | tf_op | source)
XLA Modules:
  0.0 162.5 jit_solution(9077578963030448581)
XLA Ops:
  6.4 2.6 %collective-permute-start.1 = (bf16[48,1792]{1,0:T(8,128)(2,1)S(1)}, bf16[48,1792]{1,0:T(8,128)(2,1)S(1)}, u32[]{:S(2)}, u32[]{:S(2)}) collective-permute-start(bf16[48,1792]{1,0:T(8,128)(2,1)S(1)} %get-tuple-element.34), channel_id=1, source_target_pairs={{0,8},{4,12},{8,0},{12,4},{1,9},{5,13},{9,1},{13,5},{2,10},{6,14},... | collective-permute-start | bytes 516104 | tf_op jit(solution)/shard_map/ppermute | solution.py:33
  9.2 4.8 %collective-permute-done.refs_1_ = bf16[48,1792]{1,0:T(8,128)(2,1)S(1)} collective-permute-done((bf16[48,1792]{1,0:T(8,128)(2,1)}, bf16[48,1792]{1,0:T(8,128)(2,1)S(1)}, u32[]{:S(2)}, u32[]{:S(2)}) %collective-permute-start) | collective-permute-done | bytes 172064 | tf_op jit(solution)/shard_map/ppermute | solution.py:33
  14.0 7.9 %collective-permute-done.1.refs_2_ = bf16[48,1792]{1,0:T(8,128)(2,1)S(1)} collective-permute-done((bf16[48,1792]{1,0:T(8,128)(2,1)S(1)}, bf16[48,1792]{1,0:T(8,128)(2,1)S(1)}, u32[]{:S(2)}, u32[]{:S(2)}) %collective-permute-start.1) | collective-permute-done | bytes 172064 | tf_op jit(solution)/shard_map/ppermute | solution.py:33
  22.8 11.2 %shard_map.83 = (bf16[208,512]{1,0:T(8,128)(2,1)S(1)}, bf16[208,512]{1,0:T(8,128)(2,1)S(1)}, bf16[208,512]{1,0:T(8,128)(2,1)S(1)}, bf16[208,512]{1,0:T(8,128)(2,1)S(1)}) custom-call(s32[1]{0:T(128)} %bitcast.8.h_ref, bf16[192,192]{1,0:T(8,128)(2,1)S(1)} %copy-done.3, bf16[48,1792]{1,0:T(8,128)(2,1)S(1)} %get-tuple-element.32.refs_0_, ...), custom_call_target="tpu_custom_call" | custom-call | tf_op jit(solution)/shard_map/pallas_call | solution.py:237
  36.0 6.3 %collective-permute-done.4.refs_2_ = bf16[208,512]{1,0:T(8,128)(2,1)S(1)} collective-permute-done((bf16[208,512]{1,0:T(8,128)(2,1)S(1)}, bf16[208,512]{1,0:T(8,128)(2,1)S(1)}, u32[]{:S(2)}, u32[]{:S(2)}) %collective-permute-start.4) | collective-permute-done | bytes 213024 | tf_op jit(solution)/shard_map/ppermute | solution.py:33
  42.2 3.7 %collective-permute-done.5.refs_3_ = bf16[208,512]{1,0:T(8,128)(2,1)S(1)} collective-permute-done((bf16[208,512]{1,0:T(8,128)(2,1)S(1)}, bf16[208,512]{1,0:T(8,128)(2,1)S(1)}, u32[]{:S(2)}, u32[]{:S(2)}) %collective-permute-start.5) | collective-permute-done | bytes 213024 | tf_op jit(solution)/shard_map/ppermute | solution.py:33
  48.0 2.8 %collective-permute-done.8.refs_3_ = bf16[192,256]{1,0:T(8,128)(2,1)S(1)} collective-permute-done((bf16[192,256]{1,0:T(8,128)(2,1)S(1)}, bf16[192,256]{1,0:T(8,128)(2,1)S(1)}, u32[]{:S(2)}, u32[]{:S(2)}) %collective-permute-start.8) | collective-permute-done | bytes 98336 | tf_op jit(solution)/shard_map/ppermute | solution.py:33
  50.9 2.5 %collective-permute-done.7.refs_2_ = bf16[192,256]{1,0:T(8,128)(2,1)S(1)} collective-permute-done((bf16[192,256]{1,0:T(8,128)(2,1)S(1)}, bf16[192,256]{1,0:T(8,128)(2,1)S(1)}, u32[]{:S(2)}, u32[]{:S(2)}) %collective-permute-start.7) | collective-permute-done | bytes 98336 | tf_op jit(solution)/shard_map/ppermute | solution.py:33
  53.4 5.4 %shard_map.85 = (bf16[48,1792]{1,0:T(8,128)(2,1)S(1)}, bf16[48,1792]{1,0:T(8,128)(2,1)S(1)}, bf16[48,1792]{1,0:T(8,128)(2,1)S(1)}, bf16[48,1792]{1,0:T(8,128)(2,1)S(1)}) custom-call(s32[1]{0:T(128)} %bitcast.8.h_ref, bf16[192,192]{1,0:T(8,128)(2,1)S(1)} %copy-done.3, bf16[192,256]{1,0:T(8,128)(2,1)S(1)} %shard_map.84.refs_0_, ...), custom_call_target="tpu_custom_call" | custom-call | tf_op jit(solution)/shard_map/pallas_call | solution.py:237
  58.7 2.9 %collective-permute-start.9 = (bf16[48,1792]{1,0:T(8,128)(2,1)S(1)}, bf16[48,1792]{1,0:T(8,128)(2,1)S(1)}, u32[]{:S(2)}, u32[]{:S(2)}) collective-permute-start(bf16[48,1792]{1,0:T(8,128)(2,1)S(1)} %get-tuple-element.41), channel_id=1, source_target_pairs={{0,4},{4,0},{8,12},{12,8},{1,5},{5,1},{9,13},{13,9},{2,6},{6,2},{1... | collective-permute-start | bytes 516104 | tf_op jit(solution)/shard_map/ppermute | solution.py:33
  64.1 4.4 %collective-permute-done.9.refs_1_ = bf16[48,1792]{1,0:T(8,128)(2,1)S(1)} collective-permute-done((bf16[48,1792]{1,0:T(8,128)(2,1)S(1)}, bf16[48,1792]{1,0:T(8,128)(2,1)S(1)}, u32[]{:S(2)}, u32[]{:S(2)}) %collective-permute-start.9) | collective-permute-done | bytes 172064 | tf_op jit(solution)/shard_map/ppermute | solution.py:33
  68.5 8.7 %collective-permute-done.10.refs_2_ = bf16[48,1792]{1,0:T(8,128)(2,1)S(1)} collective-permute-done((bf16[48,1792]{1,0:T(8,128)(2,1)S(1)}, bf16[48,1792]{1,0:T(8,128)(2,1)S(1)}, u32[]{:S(2)}, u32[]{:S(2)}) %collective-permute-start.10) | collective-permute-done | bytes 172064 | tf_op jit(solution)/shard_map/ppermute | solution.py:33
  79.0 6.4 %collective-permute-done.12.rows_ref = bf16[64,1792]{1,0:T(8,128)(2,1)S(1)} collective-permute-done((bf16[64,1792]{1,0:T(8,128)(2,1)S(1)}, bf16[64,1792]{1,0:T(8,128)(2,1)S(1)}, u32[]{:S(2)}, u32[]{:S(2)}) %collective-permute-start.12) | collective-permute-done | bytes 229408 | tf_op jit(solution)/shard_map/ppermute | solution.py:321
  86.1 2.8 %collective-permute-start.13 = (bf16[48,1792]{1,0:T(8,128)(2,1)S(1)}, bf16[48,1792]{1,0:T(8,128)(2,1)S(1)}, u32[]{:S(2)}, u32[]{:S(2)}) collective-permute-start(bf16[48,1792]{1,0:T(8,128)(2,1)S(1)} %get-tuple-element.46), channel_id=1, source_target_pairs={{0,4},{4,0},{8,12},{12,8},{1,5},{5,1},{9,13},{13,9},{2,6},{6,2},{1... | collective-permute-start | bytes 516104 | tf_op jit(solution)/shard_map/ppermute | solution.py:33
  93.8 8.8 %collective-permute-done.14.refs_2_ = bf16[48,1792]{1,0:T(8,128)(2,1)S(1)} collective-permute-done((bf16[48,1792]{1,0:T(8,128)(2,1)S(1)}, bf16[48,1792]{1,0:T(8,128)(2,1)S(1)}, u32[]{:S(2)}, u32[]{:S(2)}) %collective-permute-start.14) | collective-permute-done | bytes 172064 | tf_op jit(solution)/shard_map/ppermute | solution.py:33
  102.6 11.0 %shard_map.88 = (bf16[208,512]{1,0:T(8,128)(2,1)S(1)}, bf16[208,512]{1,0:T(8,128)(2,1)S(1)}, bf16[208,512]{1,0:T(8,128)(2,1)S(1)}, bf16[208,512]{1,0:T(8,128)(2,1)S(1)}) custom-call(s32[1]{0:T(128)} %bitcast.8.h_ref, bf16[192,192]{1,0:T(8,128)(2,1)S(1)} %copy-done.4, bf16[48,1792]{1,0:T(8,128)(2,1)S(1)} %get-tuple-element.45.refs_0_, ...), custom_call_target="tpu_custom_call" | custom-call | tf_op jit(solution)/shard_map/pallas_call | solution.py:237
  115.5 6.3 %collective-permute-done.17.refs_2_ = bf16[208,512]{1,0:T(8,128)(2,1)S(1)} collective-permute-done((bf16[208,512]{1,0:T(8,128)(2,1)S(1)}, bf16[208,512]{1,0:T(8,128)(2,1)S(1)}, u32[]{:S(2)}, u32[]{:S(2)}) %collective-permute-start.17) | collective-permute-done | bytes 213024 | tf_op jit(solution)/shard_map/ppermute | solution.py:33
  121.8 3.7 %collective-permute-done.18.refs_3_ = bf16[208,512]{1,0:T(8,128)(2,1)S(1)} collective-permute-done((bf16[208,512]{1,0:T(8,128)(2,1)S(1)}, bf16[208,512]{1,0:T(8,128)(2,1)S(1)}, u32[]{:S(2)}, u32[]{:S(2)}) %collective-permute-start.18) | collective-permute-done | bytes 213024 | tf_op jit(solution)/shard_map/ppermute | solution.py:33
  127.6 2.8 %collective-permute-done.21.refs_3_ = bf16[192,256]{1,0:T(8,128)(2,1)S(1)} collective-permute-done((bf16[192,256]{1,0:T(8,128)(2,1)S(1)}, bf16[192,256]{1,0:T(8,128)(2,1)S(1)}, u32[]{:S(2)}, u32[]{:S(2)}) %collective-permute-start.21) | collective-permute-done | bytes 98336 | tf_op jit(solution)/shard_map/ppermute | solution.py:33
  130.4 2.5 %collective-permute-done.20.refs_2_ = bf16[192,256]{1,0:T(8,128)(2,1)S(1)} collective-permute-done((bf16[192,256]{1,0:T(8,128)(2,1)S(1)}, bf16[192,256]{1,0:T(8,128)(2,1)S(1)}, u32[]{:S(2)}, u32[]{:S(2)}) %collective-permute-start.20) | collective-permute-done | bytes 98336 | tf_op jit(solution)/shard_map/ppermute | solution.py:33
  132.9 5.2 %copy-done = bf16[1,4096,1792]{2,1,0:T(8,128)(2,1)S(1)} copy-done((bf16[1,4096,1792]{2,1,0:T(8,128)(2,1)S(1)}, bf16[1,4096,1792]{2,1,0:T(8,128)(2,1)}, u32[]{:S(2)}) %copy-start) | copy-done | bytes 14680088
  138.1 5.3 %shard_map.90 = (bf16[48,1792]{1,0:T(8,128)(2,1)S(1)}, bf16[48,1792]{1,0:T(8,128)(2,1)S(1)}, bf16[48,1792]{1,0:T(8,128)(2,1)S(1)}, bf16[48,1792]{1,0:T(8,128)(2,1)S(1)}) custom-call(s32[1]{0:T(128)} %bitcast.8.h_ref, bf16[192,192]{1,0:T(8,128)(2,1)S(1)} %copy-done.4, bf16[192,256]{1,0:T(8,128)(2,1)S(1)} %shard_map.89.refs_0_, ...), custom_call_target="tpu_custom_call" | custom-call | tf_op jit(solution)/shard_map/pallas_call | solution.py:237
  148.8 4.1 %collective-permute-done.22.refs_1_ = bf16[48,1792]{1,0:T(8,128)(2,1)S(1)} collective-permute-done((bf16[48,1792]{1,0:T(8,128)(2,1)S(1)}, bf16[48,1792]{1,0:T(8,128)(2,1)S(1)}, u32[]{:S(2)}, u32[]{:S(2)}) %collective-permute-start.22) | collective-permute-done | bytes 172064 | tf_op jit(solution)/shard_map/ppermute | solution.py:33
  152.9 8.6 %collective-permute-done.23.refs_2_ = bf16[48,1792]{1,0:T(8,128)(2,1)S(1)} collective-permute-done((bf16[48,1792]{1,0:T(8,128)(2,1)S(1)}, bf16[48,1792]{1,0:T(8,128)(2,1)S(1)}, u32[]{:S(2)}, u32[]{:S(2)}) %collective-permute-start.23) | collective-permute-done | bytes 172064 | tf_op jit(solution)/shard_map/ppermute | solution.py:33
  (63 shorter events, 31.8 us)
Async XLA Ops:
  4.8 9.2 %collective-permute-start = (bf16[48,1792]{1,0:T(8,128)(2,1)}, bf16[48,1792]{1,0:T(8,128)(2,1)S(1)}, u32[]{:S(2)}, u32[]{:S(2)}) collective-permute-start(bf16[48,1792]{1,0:T(8,128)(2,1)} %get-tuple-element.33), channel_id=1, source_target_pairs={{0,4},{4,0},{8,12},{12,8},{1,5},{5,1},{9,13},{13,9},{2,6},{6,2},{1... | collective-permute-start | bytes 516104 | tf_op jit(solution)/shard_map/ppermute | solution.py:33
  6.4 15.6 %collective-permute-start.1 = (bf16[48,1792]{1,0:T(8,128)(2,1)S(1)}, bf16[48,1792]{1,0:T(8,128)(2,1)S(1)}, u32[]{:S(2)}, u32[]{:S(2)}) collective-permute-start(bf16[48,1792]{1,0:T(8,128)(2,1)S(1)} %get-tuple-element.34), channel_id=1, source_target_pairs={{0,8},{4,12},{8,0},{12,4},{1,9},{5,13},{9,1},{13,5},{2,10},{6,14},... | collective-permute-start | bytes 516104 | tf_op jit(solution)/shard_map/ppermute | solution.py:33
  8.9 13.0 %collective-permute-start.2 = (bf16[48,1792]{1,0:T(8,128)(2,1)S(1)}, bf16[48,1792]{1,0:T(8,128)(2,1)S(1)}, u32[]{:S(2)}, u32[]{:S(2)}) collective-permute-start(bf16[48,1792]{1,0:T(8,128)(2,1)S(1)} %get-tuple-element.35), channel_id=1, source_target_pairs={{0,12},{4,8},{8,4},{12,0},{1,13},{5,9},{9,5},{13,1},{2,14},{6,10},... | collective-permute-start | bytes 516104 | tf_op jit(solution)/shard_map/ppermute | solution.py:33
  34.0 1.9 %collective-permute-start.3 = (bf16[208,512]{1,0:T(8,128)(2,1)S(1)}, bf16[208,512]{1,0:T(8,128)(2,1)S(1)}, u32[]{:S(2)}, u32[]{:S(2)}) collective-permute-start(bf16[208,512]{1,0:T(8,128)(2,1)S(1)} %get-tuple-element.37), channel_id=1, source_target_pairs={{0,1},{1,0},{2,3},{3,2},{4,5},{5,4},{6,7},{7,6},{8,9},{9,8},{10,11... | collective-permute-start | bytes 638984 | tf_op jit(solution)/shard_map/ppermute | solution.py:33
  34.1 8.1 %collective-permute-start.4 = (bf16[208,512]{1,0:T(8,128)(2,1)S(1)}, bf16[208,512]{1,0:T(8,128)(2,1)S(1)}, u32[]{:S(2)}, u32[]{:S(2)}) collective-permute-start(bf16[208,512]{1,0:T(8,128)(2,1)S(1)} %get-tuple-element.38), channel_id=1, source_target_pairs={{0,2},{1,3},{2,0},{3,1},{4,6},{5,7},{6,4},{7,5},{8,10},{9,11},{10,... | collective-permute-start | bytes 638984 | tf_op jit(solution)/shard_map/ppermute | solution.py:33
  35.7 10.2 %collective-permute-start.5 = (bf16[208,512]{1,0:T(8,128)(2,1)S(1)}, bf16[208,512]{1,0:T(8,128)(2,1)S(1)}, u32[]{:S(2)}, u32[]{:S(2)}) collective-permute-start(bf16[208,512]{1,0:T(8,128)(2,1)S(1)} %get-tuple-element.39), channel_id=1, source_target_pairs={{0,3},{1,2},{2,1},{3,0},{4,7},{5,6},{6,5},{7,4},{8,11},{9,10},{10,... | collective-permute-start | bytes 638984 | tf_op jit(solution)/shard_map/ppermute | solution.py:33
  46.1 4.8 %collective-permute-start.8 = (bf16[192,256]{1,0:T(8,128)(2,1)S(1)}, bf16[192,256]{1,0:T(8,128)(2,1)S(1)}, u32[]{:S(2)}, u32[]{:S(2)}) collective-permute-start(bf16[192,256]{1,0:T(8,128)(2,1)S(1)} %shard_map.84.refs_0_), channel_id=1, source_target_pairs={{0,3},{1,2},{2,1},{3,0},{4,7},{5,6},{6,5},{7,4},{8,11},{9,10},{10,... | collective-permute-start | bytes 294920 | tf_op jit(solution)/shard_map/ppermute | solution.py:33
  47.5 5.8 %collective-permute-start.7 = (bf16[192,256]{1,0:T(8,128)(2,1)S(1)}, bf16[192,256]{1,0:T(8,128)(2,1)S(1)}, u32[]{:S(2)}, u32[]{:S(2)}) collective-permute-start(bf16[192,256]{1,0:T(8,128)(2,1)S(1)} %shard_map.84.refs_0_), channel_id=1, source_target_pairs={{0,2},{1,3},{2,0},{3,1},{4,6},{5,7},{6,4},{7,5},{8,10},{9,11},{10,... | collective-permute-start | bytes 294920 | tf_op jit(solution)/shard_map/ppermute | solution.py:33
  48.0 5.3 %collective-permute-start.6 = (bf16[192,256]{1,0:T(8,128)(2,1)S(1)}, bf16[192,256]{1,0:T(8,128)(2,1)S(1)}, u32[]{:S(2)}, u32[]{:S(2)}) collective-permute-start(bf16[192,256]{1,0:T(8,128)(2,1)S(1)} %shard_map.84.refs_0_), channel_id=1, source_target_pairs={{0,1},{1,0},{2,3},{3,2},{4,5},{5,4},{6,7},{7,6},{8,9},{9,8},{10,11... | collective-permute-start | bytes 294920 | tf_op jit(solution)/shard_map/ppermute | solution.py:33
  58.7 9.8 %collective-permute-start.9 = (bf16[48,1792]{1,0:T(8,128)(2,1)S(1)}, bf16[48,1792]{1,0:T(8,128)(2,1)S(1)}, u32[]{:S(2)}, u32[]{:S(2)}) collective-permute-start(bf16[48,1792]{1,0:T(8,128)(2,1)S(1)} %get-tuple-element.41), channel_id=1, source_target_pairs={{0,4},{4,0},{8,12},{12,8},{1,5},{5,1},{9,13},{13,9},{2,6},{6,2},{1... | collective-permute-start | bytes 516104 | tf_op jit(solution)/shard_map/ppermute | solution.py:33
  61.6 15.6 %collective-permute-start.10 = (bf16[48,1792]{1,0:T(8,128)(2,1)S(1)}, bf16[48,1792]{1,0:T(8,128)(2,1)S(1)}, u32[]{:S(2)}, u32[]{:S(2)}) collective-permute-start(bf16[48,1792]{1,0:T(8,128)(2,1)S(1)} %get-tuple-element.42), channel_id=1, source_target_pairs={{0,8},{4,12},{8,0},{12,4},{1,9},{5,13},{9,1},{13,5},{2,10},{6,14},... | collective-permute-start | bytes 516104 | tf_op jit(solution)/shard_map/ppermute | solution.py:33
  62.7 14.5 %collective-permute-start.11 = (bf16[48,1792]{1,0:T(8,128)(2,1)S(1)}, bf16[48,1792]{1,0:T(8,128)(2,1)S(1)}, u32[]{:S(2)}, u32[]{:S(2)}) collective-permute-start(bf16[48,1792]{1,0:T(8,128)(2,1)S(1)} %get-tuple-element.43), channel_id=1, source_target_pairs={{0,12},{4,8},{8,4},{12,0},{1,13},{5,9},{9,5},{13,1},{2,14},{6,10},... | collective-permute-start | bytes 516104 | tf_op jit(solution)/shard_map/ppermute | solution.py:33
  77.5 7.9 %collective-permute-start.12 = (bf16[64,1792]{1,0:T(8,128)(2,1)S(1)}, bf16[64,1792]{1,0:T(8,128)(2,1)S(1)}, u32[]{:S(2)}, u32[]{:S(2)}) collective-permute-start(bf16[64,1792]{1,0:T(8,128)(2,1)S(1)} %shard_map.86.kept_ref), channel_id=1, source_target_pairs={{0,16},{1,17},{2,18},{3,19},{4,20},{5,21},{6,22},{7,23},{8,24},{9,... | collective-permute-start | bytes 688136 | tf_op jit(solution)/shard_map/ppermute | solution.py:321
  86.1 7.7 %collective-permute-start.13 = (bf16[48,1792]{1,0:T(8,128)(2,1)S(1)}, bf16[48,1792]{1,0:T(8,128)(2,1)S(1)}, u32[]{:S(2)}, u32[]{:S(2)}) collective-permute-start(bf16[48,1792]{1,0:T(8,128)(2,1)S(1)} %get-tuple-element.46), channel_id=1, source_target_pairs={{0,4},{4,0},{8,12},{12,8},{1,5},{5,1},{9,13},{13,9},{2,6},{6,2},{1... | collective-permute-start | bytes 516104 | tf_op jit(solution)/shard_map/ppermute | solution.py:33
  88.9 13.6 %collective-permute-start.14 = (bf16[48,1792]{1,0:T(8,128)(2,1)S(1)}, bf16[48,1792]{1,0:T(8,128)(2,1)S(1)}, u32[]{:S(2)}, u32[]{:S(2)}) collective-permute-start(bf16[48,1792]{1,0:T(8,128)(2,1)S(1)} %get-tuple-element.47), channel_id=1, source_target_pairs={{0,8},{4,12},{8,0},{12,4},{1,9},{5,13},{9,1},{13,5},{2,10},{6,14},... | collective-permute-start | bytes 516104 | tf_op jit(solution)/shard_map/ppermute | solution.py:33
  90.2 12.3 %collective-permute-start.15 = (bf16[48,1792]{1,0:T(8,128)(2,1)S(1)}, bf16[48,1792]{1,0:T(8,128)(2,1)S(1)}, u32[]{:S(2)}, u32[]{:S(2)}) collective-permute-start(bf16[48,1792]{1,0:T(8,128)(2,1)S(1)} %get-tuple-element.48), channel_id=1, source_target_pairs={{0,12},{4,8},{8,4},{12,0},{1,13},{5,9},{9,5},{13,1},{2,14},{6,10},... | collective-permute-start | bytes 516104 | tf_op jit(solution)/shard_map/ppermute | solution.py:33
  113.7 8.1 %collective-permute-start.17 = (bf16[208,512]{1,0:T(8,128)(2,1)S(1)}, bf16[208,512]{1,0:T(8,128)(2,1)S(1)}, u32[]{:S(2)}, u32[]{:S(2)}) collective-permute-start(bf16[208,512]{1,0:T(8,128)(2,1)S(1)} %get-tuple-element.51), channel_id=1, source_target_pairs={{0,2},{1,3},{2,0},{3,1},{4,6},{5,7},{6,4},{7,5},{8,10},{9,11},{10,... | collective-permute-start | bytes 638984 | tf_op jit(solution)/shard_map/ppermute | solution.py:33
  115.3 10.2 %collective-permute-start.18 = (bf16[208,512]{1,0:T(8,128)(2,1)S(1)}, bf16[208,512]{1,0:T(8,128)(2,1)S(1)}, u32[]{:S(2)}, u32[]{:S(2)}) collective-permute-start(bf16[208,512]{1,0:T(8,128)(2,1)S(1)} %get-tuple-element.52), channel_id=1, source_target_pairs={{0,3},{1,2},{2,1},{3,0},{4,7},{5,6},{6,5},{7,4},{8,11},{9,10},{10,... | collective-permute-start | bytes 638984 | tf_op jit(solution)/shard_map/ppermute | solution.py:33
  125.7 4.8 %collective-permute-start.21 = (bf16[192,256]{1,0:T(8,128)(2,1)S(1)}, bf16[192,256]{1,0:T(8,128)(2,1)S(1)}, u32[]{:S(2)}, u32[]{:S(2)}) collective-permute-start(bf16[192,256]{1,0:T(8,128)(2,1)S(1)} %shard_map.89.refs_0_), channel_id=1, source_target_pairs={{0,3},{1,2},{2,1},{3,0},{4,7},{5,6},{6,5},{7,4},{8,11},{9,10},{10,... | collective-permute-start | bytes 294920 | tf_op jit(solution)/shard_map/ppermute | solution.py:33
  127.1 5.8 %collective-permute-start.20 = (bf16[192,256]{1,0:T(8,128)(2,1)S(1)}, bf16[192,256]{1,0:T(8,128)(2,1)S(1)}, u32[]{:S(2)}, u32[]{:S(2)}) collective-permute-start(bf16[192,256]{1,0:T(8,128)(2,1)S(1)} %shard_map.89.refs_0_), channel_id=1, source_target_pairs={{0,2},{1,3},{2,0},{3,1},{4,6},{5,7},{6,4},{7,5},{8,10},{9,11},{10,... | collective-permute-start | bytes 294920 | tf_op jit(solution)/shard_map/ppermute | solution.py:33
  127.6 5.3 %collective-permute-start.19 = (bf16[192,256]{1,0:T(8,128)(2,1)S(1)}, bf16[192,256]{1,0:T(8,128)(2,1)S(1)}, u32[]{:S(2)}, u32[]{:S(2)}) collective-permute-start(bf16[192,256]{1,0:T(8,128)(2,1)S(1)} %shard_map.89.refs_0_), channel_id=1, source_target_pairs={{0,1},{1,0},{2,3},{3,2},{4,5},{5,4},{6,7},{7,6},{8,9},{9,8},{10,11... | collective-permute-start | bytes 294920 | tf_op jit(solution)/shard_map/ppermute | solution.py:33
  143.5 9.5 %collective-permute-start.22 = (bf16[48,1792]{1,0:T(8,128)(2,1)S(1)}, bf16[48,1792]{1,0:T(8,128)(2,1)S(1)}, u32[]{:S(2)}, u32[]{:S(2)}) collective-permute-start(bf16[48,1792]{1,0:T(8,128)(2,1)S(1)} %get-tuple-element.54), channel_id=1, source_target_pairs={{0,4},{4,0},{8,12},{12,8},{1,5},{5,1},{9,13},{13,9},{2,6},{6,2},{1... | collective-permute-start | bytes 516104 | tf_op jit(solution)/shard_map/ppermute | solution.py:33
  145.9 15.6 %collective-permute-start.23 = (bf16[48,1792]{1,0:T(8,128)(2,1)S(1)}, bf16[48,1792]{1,0:T(8,128)(2,1)S(1)}, u32[]{:S(2)}, u32[]{:S(2)}) collective-permute-start(bf16[48,1792]{1,0:T(8,128)(2,1)S(1)} %get-tuple-element.55), channel_id=1, source_target_pairs={{0,8},{4,12},{8,0},{12,4},{1,9},{5,13},{9,1},{13,5},{2,10},{6,14},... | collective-permute-start | bytes 516104 | tf_op jit(solution)/shard_map/ppermute | solution.py:33
  147.4 14.0 %collective-permute-start.24 = (bf16[48,1792]{1,0:T(8,128)(2,1)S(1)}, bf16[48,1792]{1,0:T(8,128)(2,1)S(1)}, u32[]{:S(2)}, u32[]{:S(2)}) collective-permute-start(bf16[48,1792]{1,0:T(8,128)(2,1)S(1)} %get-tuple-element.56), channel_id=1, source_target_pairs={{0,12},{4,8},{8,4},{12,0},{1,13},{5,9},{9,5},{13,1},{2,14},{6,10},... | collective-permute-start | bytes 516104 | tf_op jit(solution)/shard_map/ppermute | solution.py:33
  (12 other events, 370.8 us)

commit v2 on v0

v2 whole, which is shorter than its diff:
```python
import functools

import jax
import jax.numpy as jnp
from jax import lax
from jax.experimental import pallas as pl
from jax.experimental.pallas import tpu as pltpu
from jax.sharding import PartitionSpec as P

D = 7168
FFE = 1024
CAP = 3
EPS = 1e-06
EXTRA = 16
VMEM = pl.BlockSpec(memory_space=pltpu.VMEM)
HBM = pl.BlockSpec(memory_space=pltpu.HBM)
BF16 = jnp.bfloat16
F32 = jnp.float32
I32 = jnp.int32
ACROSS = (((1,), (1,)), ((), ()))
DOWN = (((0,), (0,)), ((), ()))


def padded(count, unit):
    return -(-count // unit) * unit


def dot(a, b, dims=(((1,), (0,)), ((), ()))):
    return lax.dot_general(a, b, dims, preferred_element_type=F32)


def one_hot(mask):
    return jnp.where(mask, F32(1.0), F32(0.0))


def divided(value, divisor):
    if divisor == 1:
        return value, jnp.zeros_like(value)
    quotient = lax.shift_right_logical(value * (2**20 // divisor + 1), 20)
    return quotient, value - quotient * divisor


class Sizes:
    def __init__(self, tokens, gate_up, peers, splits):
        self.peers, self.splits = peers, splits
        self.micro, self.tok, self.width = tokens.shape
        self.rows = self.micro * self.tok
        self.units_dev = gate_up.shape[3]
        self.units = min(FFE, self.units_dev)
        self.half = self.units // 2
        self.local = self.units_dev // self.units
        self.groups = 2 if self.local % 2 == 0 else 1
        self.members = self.local // self.groups
        self.slots = self.micro * CAP
        self.pay = padded(self.members * self.slots, 8)
        self.pieces = peers if peers <= 8 else 1
        self.group_pay = peers * self.pay
        self.piece = self.group_pay // self.pieces
        self.all_pay = self.groups * self.group_pay
        self.each = padded(peers * self.slots, 8)
        self.group_each = self.members * self.each
        self.partial = (self.group_each + EXTRA, 2 * self.half)

    def order(self):
        shape = (self.group_each, self.group_pay)
        row = lax.broadcasted_iota(I32, (self.group_each, 1), 0)
        expert, rest = divided(row, self.each)
        step, slot = divided(rest, self.slots)
        target = jnp.where(step < self.peers, step * self.pay + expert * self.slots + slot, -1)
        return one_hot(lax.broadcasted_iota(I32, shape, 1) == target).astype(BF16)


def line_up(z, ref):
    total = None
    for batch in range(z.micro):
        shape = (z.tok, z.rows)
        place = lax.broadcasted_iota(I32, shape, 1) == lax.broadcasted_iota(I32, shape, 0) + batch * z.tok
        value = dot(ref[batch].astype(F32).astype(BF16), one_hot(place).astype(BF16))
        total = value if total is None else total + value
    return total


def slot_hits(z, routes_ref):
    row = lax.broadcasted_iota(I32, (z.all_pay, 1), 0)
    group, rest = divided(row, z.group_pay)
    step, place = divided(rest, z.pay)
    member, inside = divided(place, z.slots)
    batch, rank = divided(inside, CAP)
    rank = jnp.where(member < z.members, rank, -1)
    owner = step ^ lax.axis_index("expert") if z.pieces > 1 else step
    if z.units_dev >= FFE:
        expert = owner * z.local + group * z.members + member
    else:
        expert = lax.shift_right_logical(owner, (FFE // z.units_dev).bit_length() - 1)
    routes = line_up(z, routes_ref)
    token = lax.broadcasted_iota(I32, (z.all_pay, z.rows), 1)
    start = batch * z.tok
    same = (token >= start) & (token < start + z.tok)
    expert = expert.astype(F32)
    first = (routes[0:1, :] == expert) & same
    second = (routes[1:2, :] == expert) & same
    chosen = one_hot(first | second)
    shape = (z.rows, z.rows)
    before = lax.broadcasted_iota(I32, shape, 0) < lax.broadcasted_iota(I32, shape, 1)
    count = dot(chosen.astype(BF16), one_hot(before).astype(BF16))
    hits = jnp.where(count == rank.astype(F32), chosen, F32(0.0))
    return hits, first, second


def send_rows(z, hits, rows, outs):
    value = dot(hits.astype(BF16), rows)
    for index, out in enumerate(outs):
        out[...] = value[index * z.piece:(index + 1) * z.piece].astype(BF16)


def pack_kernel(z, routes_ref, gates_ref, rows_ref, *outs):
    hits, first, second = slot_hits(z, routes_ref)
    gates = line_up(z, gates_ref)
    weight = jnp.where(first, gates[0:1, :], F32(0.0)) + jnp.where(second, gates[1:2, :], F32(0.0))
    outs[-1][...] = (hits * weight).astype(BF16)
    send_rows(z, hits, rows_ref[...], outs[:-1])


def load_kernel(z, parts, experts, after, gate_up, *refs):
    outs, sems = refs[:-1], refs[-1]
    flat = gate_up.reshape(2 * z.width, z.units_dev)
    depth = 2 * z.width // parts
    copies = []
    for index, expert in enumerate(experts):
        for part in range(parts):
            copies.append(
                pltpu.make_async_copy(
                    flat.at[pl.ds(part * depth, depth), pl.ds(expert * z.units, z.units)],
                    outs[index].at[pl.ds(part * depth, depth)],
                    sems.at[index * parts + part],
                )
            )
    for copy in copies:
        copy.start()
    for copy in copies:
        copy.wait()


def load_down_kernel(z, experts, after, down_proj, *refs):
    outs, sems = refs[:-1], refs[-1]
    copies = [
        pltpu.make_async_copy(
            down_proj.at[0, pl.ds(expert * z.units, z.units), :], outs[index], sems.at[index]
        )
        for index, expert in enumerate(experts)
    ]
    for copy in copies:
        copy.start()
    for copy in copies:
        copy.wait()


def split_sums(sums, lanes):
    high = sums.astype(BF16).astype(F32)
    row = lax.broadcasted_iota(I32, sums.shape, 0)
    both = jnp.where(row == 0, high, jnp.where(row == 1, sums - high, F32(0.0)))
    if both.shape[1] < lanes:
        both = jnp.concatenate([both, jnp.zeros((EXTRA, lanes - both.shape[1]), F32)], axis=1)
    return both


def up_kernel(z, *refs):
    weights, refs = refs[:z.members], refs[z.members:]
    received, refs = refs[:z.pieces], refs[z.pieces:]
    own, sent, spread, staged = refs
    stacked = jnp.concatenate([piece[...].astype(F32) for piece in received], axis=0).astype(BF16)
    rows = dot(z.order(), stacked)
    squares = rows * rows
    high = squares.astype(BF16)
    low = (squares - high.astype(F32)).astype(BF16)
    ones = jnp.ones((EXTRA, z.width), BF16)
    sums = dot(ones, high, ACROSS) + dot(ones, low, ACROSS)
    rows = rows.astype(BF16)
    block = 128
    shape = (block, 2 * block)
    target = lax.broadcasted_iota(I32, shape, 1) - 2 * lax.broadcasted_iota(I32, shape, 0)
    placing = [one_hot(target == side).astype(BF16) for side in range(2)]
    for piece in range(z.width // block):
        columns = slice(piece * block, (piece + 1) * block)
        gate, up = dot(rows[:, columns], placing[0]), dot(rows[:, columns], placing[1])
        for expert in range(z.members):
            here = slice(expert * z.each, (expert + 1) * z.each)
            both = jnp.concatenate([gate[here], up[here]], axis=0).astype(BF16)
            spread[expert, :, 2 * piece * block:2 * (piece + 1) * block] = both
    totals = [dot(spread[expert], weights[expert][...]) for expert in range(z.members)]
    extra = split_sums(sums, 2 * z.half)
    for side in range(2):
        columns = slice(side * z.half, (side + 1) * z.half)
        gate = jnp.concatenate([total[:z.each, columns] for total in totals], axis=0)
        up = jnp.concatenate([total[z.each:, columns] for total in totals], axis=0)
        staged[side, :z.group_each, :] = jnp.concatenate([gate, up], axis=1)
        staged[side, z.group_each:, :] = extra
    core = lax.axis_index("hidden") & 1
    own[...] = staged[core]
    sent[...] = staged[1 - core].astype(BF16)


def joined(z, refs):
    total = refs[0][...].astype(F32)
    for ref in refs[1:]:
        total = total + ref[...].astype(F32)
    products, extra = total[:z.group_each], total[z.group_each:]
    row = lax.broadcasted_iota(I32, extra.shape, 0)
    sums = jnp.sum(jnp.where(row < 2, extra, F32(0.0)), axis=0, keepdims=True)
    return products, sums


def pair_kernel(z, own, other, out):
    products, sums = joined(z, (own, other))
    out[:z.group_each, :] = products.astype(BF16)
    sums = jnp.broadcast_to(sums, (EXTRA, 2 * z.half))
    out[z.group_each:, :] = split_sums(sums, 2 * z.half).astype(BF16)


def act_kernel(z, *refs):
    out = refs[-1]
    products, sums = joined(z, refs[:-1])
    shape = (z.group_each, z.group_each)
    diagonal = lax.broadcasted_iota(I32, shape, 0) == lax.broadcasted_iota(I32, shape, 1)
    sums = jnp.sum(jnp.where(diagonal, sums[:, :z.group_each], F32(0.0)), axis=1, keepdims=True)
    scale = lax.rsqrt(sums / D + EPS)
    gate = scale * products[:, :z.half]
    up = scale * products[:, z.half:]
    out[...] = (gate / (F32(1.0) + jnp.exp(-gate)) * up).astype(BF16)


def down_kernel(z, *refs):
    weights, refs = refs[:z.members], refs[z.members:]
    halves, outs = refs[:2], refs[2:]
    core = lax.axis_index("hidden") & 1
    results = []
    for expert in range(z.members):
        total = None
        for step in range(2):
            units = halves[step][...].astype(F32)[expert * z.each:(expert + 1) * z.each].astype(BF16)
            low = pl.multiple_of((core ^ step) * z.half, z.half)
            value = dot(units, weights[expert][pl.ds(low, z.half), :])
            total = value if total is None else total + value
        results.append(total)
    value = dot(z.order(), jnp.concatenate(results, axis=0).astype(BF16), DOWN)
    for index, out in enumerate(outs):
        out[...] = value[index * z.piece:(index + 1) * z.piece].astype(BF16)


def combine_kernel(z, tick, last, weight_ref, rows_ref, kept_ref, *refs):
    count = z.groups * z.pieces
    returned, refs = refs[:count], refs[count:]
    stacked = jnp.concatenate([piece[...].astype(F32) for piece in returned], axis=0).astype(BF16)
    mixed = dot(weight_ref[...], stacked, DOWN)
    value = (rows_ref[...].astype(F32) + mixed).astype(BF16)
    if last:
        refs[0][...] = jnp.where(lax.axis_index("section") == tick, value, kept_ref[...])
        return
    routes_ref, out, outs = refs[0], refs[1], refs[2:]
    out[...] = jnp.where(lax.axis_index("section") == tick, value, kept_ref[...])
    hits, _, _ = slot_hits(z, routes_ref)
    send_rows(z, hits, value, outs)


def call(kernel, sizes, megabytes, cost, outs, in_specs, scratch, *args):
    flops, moved = cost
    results = pl.pallas_call(
        functools.partial(kernel, *sizes),
        out_shape=outs,
        in_specs=in_specs,
        out_specs=[VMEM] * len(outs),
        scratch_shapes=scratch,
        compiler_params=pltpu.CompilerParams(vmem_limit_bytes=megabytes * 2**20),
        cost_estimate=pl.CostEstimate(flops=flops, bytes_accessed=moved, transcendentals=0),
    )(*args)
    return list(results)


def on_device(tokens, gate_up, down_proj, routes, gate_weights):
    sections = lax.axis_size("section")
    z = Sizes(tokens, gate_up, lax.axis_size("expert"), lax.axis_size("hidden"))
    parts = 2 if z.width % 256 == 0 else 1
    shape = jax.ShapeDtypeStruct
    pay = shape((z.piece, z.width), BF16)
    whole = shape((z.rows, z.width), BF16)
    steps = sorted(range(z.peers), key=lambda step: -step.bit_length())
    second = 10**6

    def swap(value, step):
        pairs = [(i, i ^ step) for i in range(z.splits)]
        return lax.ppermute(value, "hidden", pairs)

    def exchanged(pieces):
        if z.pieces == 1:
            return [lax.all_to_all(pieces[0], "expert", split_axis=0, concat_axis=0, tiled=True)]
        result = list(pieces)
        for step in steps[:-1]:
            pairs = [(i, i ^ step) for i in range(z.peers)]
            result[step] = lax.ppermute(pieces[step], "expert", pairs)
        return result

    def relayed(pieces, tick):
        if z.pieces == 1:
            return [lax.ppermute(exchanged(pieces)[0], "section", [(tick, tick + 1)])]
        result = list(pieces)
        for step in steps:
            pairs = [(tick * z.peers + i, (tick + 1) * z.peers + (i ^ step)) for i in range(z.peers)]
            result[step] = lax.ppermute(pieces[step], ("section", "expert"), pairs)
        return result

    def grouped(pieces):
        return [pieces[group * z.pieces:(group + 1) * z.pieces] for group in range(z.groups)]

    def middle(received, wide):
        own, sent = call(
            up_kernel, (z,), 6, (0, 3 * second * 3),
            [shape(z.partial, F32), shape(z.partial, BF16)],
            [VMEM] * (z.members + z.pieces),
            [
                pltpu.VMEM((z.members, 2 * z.each, 2 * z.width), BF16),
                pltpu.VMEM((2,) + z.partial, F32),
            ],
            *wide, *received,
        )
        pair = call(
            pair_kernel, (z,), 2, (0, second), [shape(z.partial, BF16)], [VMEM] * 2, [],
            own, swap(sent, 1),
        )[0]
        pairs = [pair] + [swap(pair, step) for step in range(2, z.splits, 2)]
        units = call(
            act_kernel, (z,), 2, (0, second),
            [shape((z.group_each, z.half), BF16)], [VMEM] * len(pairs), [], *pairs,
        )[0]
        return units, swap(units, 1)

    def after(halves, tall):
        return call(
            down_kernel, (z,), 4, (0, 3 * second * 2), [pay] * z.pieces, [VMEM] * (z.members + 2), [],
            *tall, *halves,
        )

    routes = routes[0].transpose(0, 2, 1)
    gates = gate_weights[0].transpose(0, 2, 1)
    rows = tokens.reshape(z.rows, z.width)
    kept = rows
    *sent, weight = call(
        pack_kernel, (z,), 3, (0, second),
        [pay] * (z.groups * z.pieces) + [shape((z.all_pay, z.rows), BF16)],
        [VMEM] * 3, [], routes, gates, rows,
    )
    received = [exchanged(pieces) for pieces in grouped(sent)]
    following = lax.ppermute(routes, "section", [(i + 1, i) for i in range(sections - 1)])
    gate_up = pltpu.with_memory_space_constraint(gate_up, pltpu.HBM)
    down_proj = pltpu.with_memory_space_constraint(down_proj, pltpu.HBM)
    wide, tall = [], []
    for group in range(z.groups):
        experts = range(group * z.members, (group + 1) * z.members)
        wide.append(call(
            load_kernel, (z, parts, experts), 1, (0, 5 * second * 3),
            [pltpu.VMEM((2 * z.width, z.units), BF16)] * z.members, [VMEM, HBM],
            [pltpu.SemaphoreType.DMA((z.members * parts,))],
            weight, gate_up,
        ))
    for group in range(z.groups):
        experts = range(group * z.members, (group + 1) * z.members)
        tall.append(call(
            load_down_kernel, (z, experts), 1, (0, 2 * second * 3),
            [pltpu.VMEM((z.units, z.width), BF16)] * z.members, [VMEM, HBM],
            [pltpu.SemaphoreType.DMA((z.members,))],
            weight, down_proj,
        ))
    for tick in range(sections):
        halves = [middle(received[group], wide[group]) for group in range(z.groups)]
        returned = []
        for group in range(z.groups):
            returned += exchanged(after(halves[group], tall[group]))
        last = tick == sections - 1
        kept, *sent = call(
            combine_kernel, (z, tick, last), 4, (0, second),
            [whole] if last else [whole] + [pay] * (z.groups * z.pieces),
            [VMEM] * (3 + len(returned) + (not last)), [],
            weight, rows, kept, *returned, *([] if last else [following]),
        )
        if not last:
            received = [relayed(pieces, tick) for pieces in grouped(sent)]
            rows = lax.ppermute(kept, "section", [(tick, tick + 1)])
    return kept.reshape(1, z.micro, z.tok, z.width)


def solution(mesh):
    placed = (
        P(None, "expert", "hidden"),
        P("section", "hidden", None, "expert"),
        P("section", "expert", "hidden"),
        P("section", None, "expert", None),
        P("section", None, "expert", None),
    )
    return jax.shard_map(
        on_device,
        mesh=mesh,
        in_specs=placed,
        out_specs=P("section", None, "expert", "hidden"),
        check_vma=False,
    )
```

time: 549 us -> 136 us (0.25)
  local copies, waits for them, and re-layouts: 161 us -> 2.32 us
  blocking collectives: 106 us -> 0 us
  matrix products: 99.3 us -> 0 us
  waiting for transfers between devices: 119 us -> 44.1 us
  Pallas kernels: 0 us -> 39.2 us
  starting transfers between devices: 29.7 us -> 49 us
  other arithmetic: 13.8 us -> 0 us
  between operations: 13.1 us -> 0.42 us
    dot_general x20 -> x0, matrix products: 99.3 us -> none  [the longest x5 61.1 us: expert_outputs(): jnp.einsum('jrd,jdf->jrf', expert_rows, w_in, preferred_element_type=jnp....]
    another operation x2 -> x0, local copies, waits for them, and re-layouts: 97.5 us -> none  [on_device(): w_in.reshape(slice_width, 2, local_count, splits, local_units // splits)]
    reduce_scatter x5 -> x0, waiting for transfers between devices: 59.4 us -> none  [expert_outputs(): lax.psum_scatter(projected, 'hidden', scatter_dimension=2, tiled=True)]
    all_to_all x5 -> x0, blocking collectives: 49.4 us -> none  [run_layer(): lax.all_to_all(sent, 'expert', split_axis=0, concat_axis=0, tiled=True)]
    reshape x1 -> x0, local copies, waits for them, and re-layouts: 47.7 us -> none  [on_device(): w_in = w_in.reshape(local_count, slice_width, 2 * local_units)]
    ppermute x5 -> x40, starting transfers between devices: 6.46 us -> 49 us  [the longest x18 28.1 us: exchanged(): result[step] = lax.ppermute(pieces[step], 'expert', pairs)]
    all_to_all x5 -> x0, waiting for transfers between devices: 42.2 us -> none  [run_layer(): lax.all_to_all(outgoing, 'expert', split_axis=0, concat_axis=0, tiled=True)]
    pallas_call x0 -> x23, Pallas kernels: none -> 39.2 us  [call(): pl.pallas_call(functools.partial(kernel, *sizes), out_shape=outs, in_spec...]
  transfers between devices with their start and end apart: 15 -> 40, of which waited for: 15 -> 13; matrix products, arithmetic and copies ran while one was open for 3% -> 0% of each run, Pallas kernels for 0% -> 27%
where the time goes in v2:
time: 136 us; the launch traced here: 135 us
  starting transfers between devices  49 us (36%)
  waiting for transfers between devices  44.1 us (32%)
  Pallas kernels  39.2 us (29%)
  local copies, waits for them, and re-layouts  2.32 us (2%)
    pallas_call x23, Pallas kernels, call(): pl.pallas_call(functools.partial(kernel, *sizes), out_shape=outs, in_spec...  39.2 us
    ppermute x18, starting transfers between devices, exchanged(): result[step] = lax.ppermute(pieces[step], 'expert', pairs)  28.1 us
    ppermute x12, waiting for transfers between devices, swap(): return lax.ppermute(value, 'hidden', pairs)  17.9 us
    ppermute x18, waiting for transfers between devices, exchanged(): result[step] = lax.ppermute(pieces[step], 'expert', pairs)  14.8 us
    ppermute x8, waiting for transfers between devices, relayed(): result[step] = lax.ppermute(pieces[step], ('section', 'expert'), pairs)  11.4 us
    ppermute x8, starting transfers between devices, relayed(): result[step] = lax.ppermute(pieces[step], ('section', 'expert'), pairs)  10.5 us
    ppermute x12, starting transfers between devices, swap(): return lax.ppermute(value, 'hidden', pairs)  6.69 us
  transfers between devices with their start and end apart: 40, of which 13 were waited for; matrix products, arithmetic and copies ran while one was open for 0% of the time, Pallas kernels for 27%

profile of v2, /device:TPU:2, one launch (start us, length us, event | category | flops | bytes accessed | tf_op | source)
XLA Modules:
  0.0 135.1 jit_solution(13975808619949961383)
XLA Ops:
  4.6 2.6 %collective-permute-start.10 = (bf16[24,1792]{1,0:T(8,128)(2,1)S(1)}, bf16[24,1792]{1,0:T(8,128)(2,1)S(1)}, u32[]{:S(2)}, u32[]{:S(2)}) collective-permute-start(bf16[24,1792]{1,0:T(8,128)(2,1)S(1)} %get-tuple-element.76), channel_id=1, source_target_pairs={{0,8},{4,12},{8,0},{12,4},{1,9},{5,13},{9,1},{13,5},{2,10},{6,14},... | collective-permute-start | bytes 258056 | tf_op jit(solution)/shard_map/ppermute | solution.py:299
  8.1 3.5 %collective-permute-start.1 = (bf16[24,1792]{1,0:T(8,128)(2,1)S(1)}, bf16[24,1792]{1,0:T(8,128)(2,1)S(1)}, u32[]{:S(2)}, u32[]{:S(2)}) collective-permute-start(bf16[24,1792]{1,0:T(8,128)(2,1)S(1)} %get-tuple-element.62), channel_id=1, source_target_pairs={{0,8},{4,12},{8,0},{12,4},{1,9},{5,13},{9,1},{13,5},{2,10},{6,14},... | collective-permute-start | bytes 258056 | tf_op jit(solution)/shard_map/ppermute | solution.py:299
  12.0 5.4 %shard_map.63 = (bf16[3584,1024]{1,0:T(8,128)(2,1)S(1)}, bf16[3584,1024]{1,0:T(8,128)(2,1)S(1)}) custom-call(bf16[192,64]{1,0:T(8,128)(2,1)S(1)} %get-tuple-element.55.after.weight_ref, bf16[1,1792,2,4096]{3,2,1,0:T(2,128)(2,1)} %gate_up.3), custom_call_target="tpu_custom_call" | custom-call | bytes 15000000 | tf_op jit(solution)/shard_map/pallas_call | solution.py:267
  17.3 3.2 %shard_map.64 = (f32[112,1024]{1,0:T(8,128)S(1)}, bf16[112,1024]{1,0:T(8,128)(2,1)S(1)}) custom-call(bf16[3584,1024]{1,0:T(8,128)(2,1)S(1)} %get-tuple-element.72.refs_0_, bf16[3584,1024]{1,0:T(8,128)(2,1)S(1)} %get-tuple-element.73.refs_1_, bf16[24,1792]{1,0:T(8,128)(2,1)S(1)} %get-tuple-element.74.refs_2_, ...), custom_call_target="tpu_custom_call" | custom-call | bytes 9000000 | tf_op jit(solution)/shard_map/pallas_call | solution.py:267
  20.6 5.4 %shard_map.57 = (bf16[3584,1024]{1,0:T(8,128)(2,1)S(1)}, bf16[3584,1024]{1,0:T(8,128)(2,1)S(1)}) custom-call(bf16[192,64]{1,0:T(8,128)(2,1)S(1)} %get-tuple-element.55.after.weight_ref, bf16[1,1792,2,4096]{3,2,1,0:T(2,128)(2,1)} %gate_up.3), custom_call_target="tpu_custom_call" | custom-call | bytes 15000000 | tf_op jit(solution)/shard_map/pallas_call | solution.py:267
  26.0 3.2 %shard_map.58 = (f32[112,1024]{1,0:T(8,128)S(1)}, bf16[112,1024]{1,0:T(8,128)(2,1)S(1)}) custom-call(bf16[3584,1024]{1,0:T(8,128)(2,1)S(1)} %get-tuple-element.58.refs_0_, bf16[3584,1024]{1,0:T(8,128)(2,1)S(1)} %get-tuple-element.59.refs_1_, bf16[24,1792]{1,0:T(8,128)(2,1)S(1)} %get-tuple-element.60.refs_2_, ...), custom_call_target="tpu_custom_call" | custom-call | bytes 9000000 | tf_op jit(solution)/shard_map/pallas_call | solution.py:267
  32.5 5.8 %collective-permute-done.13.refs_1_ = bf16[112,1024]{1,0:T(8,128)(2,1)S(1)} collective-permute-done((bf16[112,1024]{1,0:T(8,128)(2,1)S(1)}, bf16[112,1024]{1,0:T(8,128)(2,1)S(1)}, u32[]{:S(2)}, u32[]{:S(2)}) %collective-permute-start.13) | collective-permute-done | bytes 229408 | tf_op jit(solution)/shard_map/ppermute | solution.py:291
  38.6 3.7 %collective-permute-done.4.refs_1_ = bf16[112,1024]{1,0:T(8,128)(2,1)S(1)} collective-permute-done((bf16[112,1024]{1,0:T(8,128)(2,1)S(1)}, bf16[112,1024]{1,0:T(8,128)(2,1)S(1)}, u32[]{:S(2)}, u32[]{:S(2)}) %collective-permute-start.4) | collective-permute-done | bytes 229408 | tf_op jit(solution)/shard_map/ppermute | solution.py:291
  42.6 3.2 %shard_map.62 = (bf16[1024,1792]{1,0:T(8,128)(2,1)S(1)}, bf16[1024,1792]{1,0:T(8,128)(2,1)S(1)}) custom-call(bf16[192,64]{1,0:T(8,128)(2,1)S(1)} %get-tuple-element.55.after.weight_ref, bf16[1,4096,1792]{2,1,0:T(8,128)(2,1)} %down_proj.3), custom_call_target="tpu_custom_call" | custom-call | bytes 6000000 | tf_op jit(solution)/shard_map/pallas_call | solution.py:267
  47.3 3.0 %collective-permute-start.15 = (bf16[24,1792]{1,0:T(8,128)(2,1)S(1)}, bf16[24,1792]{1,0:T(8,128)(2,1)S(1)}, u32[]{:S(2)}, u32[]{:S(2)}) collective-permute-start(bf16[24,1792]{1,0:T(8,128)(2,1)S(1)} %get-tuple-element.81), channel_id=1, source_target_pairs={{0,4},{4,0},{8,12},{12,8},{1,5},{5,1},{9,13},{13,9},{2,6},{6,2},{1... | collective-permute-start | bytes 258056 | tf_op jit(solution)/shard_map/ppermute | solution.py:299
  50.3 2.4 %collective-permute-start.18 = (s32[4,2,16]{2,1,0:T(2,128)S(1)}, s32[4,2,16]{2,1,0:T(2,128)S(1)}, u32[]{:S(2)}, u32[]{:S(2)}) collective-permute-start(s32[4,2,16]{2,1,0:T(2,128)S(1)} %bitcast.12), channel_id=1, source_target_pairs={{16,0},{17,1},{18,2},{19,3},{20,4},{21,5},{22,6},{23,7},{24,8},{25... | collective-permute-start | bytes 1544 | tf_op jit(solution)/shard_map/ppermute | solution.py:352
  52.8 3.2 %shard_map.56 = (bf16[1024,1792]{1,0:T(8,128)(2,1)S(1)}, bf16[1024,1792]{1,0:T(8,128)(2,1)S(1)}) custom-call(bf16[192,64]{1,0:T(8,128)(2,1)S(1)} %get-tuple-element.55.after.weight_ref, bf16[1,4096,1792]{2,1,0:T(8,128)(2,1)} %down_proj.3), custom_call_target="tpu_custom_call" | custom-call | bytes 6000000 | tf_op jit(solution)/shard_map/pallas_call | solution.py:267
  61.1 2.1 %collective-permute-start.7 = (bf16[24,1792]{1,0:T(8,128)(2,1)S(1)}, bf16[24,1792]{1,0:T(8,128)(2,1)S(1)}, u32[]{:S(2)}, u32[]{:S(2)}) collective-permute-start(bf16[24,1792]{1,0:T(8,128)(2,1)S(1)} %get-tuple-element.68), channel_id=1, source_target_pairs={{0,8},{4,12},{8,0},{12,4},{1,9},{5,13},{9,1},{13,5},{2,10},{6,14},... | collective-permute-start | bytes 258056 | tf_op jit(solution)/shard_map/ppermute | solution.py:299
  66.8 5.7 %collective-permute-done.7.refs_2_ = bf16[24,1792]{1,0:T(8,128)(2,1)S(1)} collective-permute-done((bf16[24,1792]{1,0:T(8,128)(2,1)S(1)}, bf16[24,1792]{1,0:T(8,128)(2,1)S(1)}, u32[]{:S(2)}, u32[]{:S(2)}) %collective-permute-start.7) | collective-permute-done | bytes 86048 | tf_op jit(solution)/shard_map/ppermute | solution.py:299
  84.0 5.5 %collective-permute-done.32.refs_4_ = bf16[24,1792]{1,0:T(8,128)(2,1)S(1)} collective-permute-done((bf16[24,1792]{1,0:T(8,128)(2,1)S(1)}, bf16[24,1792]{1,0:T(8,128)(2,1)S(1)}, u32[]{:S(2)}, u32[]{:S(2)}) %collective-permute-start.32) | collective-permute-done | bytes 86048 | tf_op jit(solution)/shard_map/ppermute | solution.py:308
  90.9 3.2 %shard_map.73 = (f32[112,1024]{1,0:T(8,128)S(1)}, bf16[112,1024]{1,0:T(8,128)(2,1)S(1)}) custom-call(bf16[3584,1024]{1,0:T(8,128)(2,1)S(1)} %get-tuple-element.72.refs_0_, bf16[3584,1024]{1,0:T(8,128)(2,1)S(1)} %get-tuple-element.73.refs_1_, bf16[24,1792]{1,0:T(8,128)(2,1)S(1)} %collective-permute-done.30.refs_2_, ...), custom_call_target="tpu_custom_call" | custom-call | bytes 9000000 | tf_op jit(solution)/shard_map/pallas_call | solution.py:267
  94.2 2.2 %collective-permute-done.22.refs_4_ = bf16[24,1792]{1,0:T(8,128)(2,1)S(1)} collective-permute-done((bf16[24,1792]{1,0:T(8,128)(2,1)S(1)}, bf16[24,1792]{1,0:T(8,128)(2,1)S(1)}, u32[]{:S(2)}, u32[]{:S(2)}) %collective-permute-start.22) | collective-permute-done | bytes 86048 | tf_op jit(solution)/shard_map/ppermute | solution.py:308
  96.4 2.1 %collective-permute-done.23.refs_5_ = bf16[24,1792]{1,0:T(8,128)(2,1)S(1)} collective-permute-done((bf16[24,1792]{1,0:T(8,128)(2,1)S(1)}, bf16[24,1792]{1,0:T(8,128)(2,1)S(1)}, u32[]{:S(2)}, u32[]{:S(2)}) %collective-permute-start.23) | collective-permute-done | bytes 86048 | tf_op jit(solution)/shard_map/ppermute | solution.py:308
  98.5 3.2 %shard_map.69 = (f32[112,1024]{1,0:T(8,128)S(1)}, bf16[112,1024]{1,0:T(8,128)(2,1)S(1)}) custom-call(bf16[3584,1024]{1,0:T(8,128)(2,1)S(1)} %get-tuple-element.58.refs_0_, bf16[3584,1024]{1,0:T(8,128)(2,1)S(1)} %get-tuple-element.59.refs_1_, bf16[24,1792]{1,0:T(8,128)(2,1)S(1)} %collective-permute-done.20.refs_2_, ...), custom_call_target="tpu_custom_call" | custom-call | bytes 9000000 | tf_op jit(solution)/shard_map/pallas_call | solution.py:267
  106.2 4.1 %collective-permute-done.35.refs_1_ = bf16[112,1024]{1,0:T(8,128)(2,1)S(1)} collective-permute-done((bf16[112,1024]{1,0:T(8,128)(2,1)S(1)}, bf16[112,1024]{1,0:T(8,128)(2,1)S(1)}, u32[]{:S(2)}, u32[]{:S(2)}) %collective-permute-start.35) | collective-permute-done | bytes 229408 | tf_op jit(solution)/shard_map/ppermute | solution.py:291
  110.5 4.2 %collective-permute-done.25.refs_1_ = bf16[112,1024]{1,0:T(8,128)(2,1)S(1)} collective-permute-done((bf16[112,1024]{1,0:T(8,128)(2,1)S(1)}, bf16[112,1024]{1,0:T(8,128)(2,1)S(1)}, u32[]{:S(2)}, u32[]{:S(2)}) %collective-permute-start.25) | collective-permute-done | bytes 229408 | tf_op jit(solution)/shard_map/ppermute | solution.py:291
  117.9 3.2 %collective-permute-start.39 = (bf16[24,1792]{1,0:T(8,128)(2,1)S(1)}, bf16[24,1792]{1,0:T(8,128)(2,1)S(1)}, u32[]{:S(2)}, u32[]{:S(2)}) collective-permute-start(bf16[24,1792]{1,0:T(8,128)(2,1)S(1)} %get-tuple-element.104), channel_id=1, source_target_pairs={{0,12},{4,8},{8,4},{12,0},{1,13},{5,9},{9,5},{13,1},{2,14},{6,10},... | collective-permute-start | bytes 258056 | tf_op jit(solution)/shard_map/ppermute | solution.py:299
  123.9 3.2 %collective-permute-start.29 = (bf16[24,1792]{1,0:T(8,128)(2,1)S(1)}, bf16[24,1792]{1,0:T(8,128)(2,1)S(1)}, u32[]{:S(2)}, u32[]{:S(2)}) collective-permute-start(bf16[24,1792]{1,0:T(8,128)(2,1)S(1)} %get-tuple-element.94), channel_id=1, source_target_pairs={{0,12},{4,8},{8,4},{12,0},{1,13},{5,9},{9,5},{13,1},{2,14},{6,10},... | collective-permute-start | bytes 258056 | tf_op jit(solution)/shard_map/ppermute | solution.py:299
  128.2 5.9 %collective-permute-done.28.refs_2_ = bf16[24,1792]{1,0:T(8,128)(2,1)S(1)} collective-permute-done((bf16[24,1792]{1,0:T(8,128)(2,1)S(1)}, bf16[24,1792]{1,0:T(8,128)(2,1)S(1)}, u32[]{:S(2)}, u32[]{:S(2)}) %collective-permute-start.28) | collective-permute-done | bytes 86048 | tf_op jit(solution)/shard_map/ppermute | solution.py:299
  (89 shorter events, 45.6 us)
Async XLA Ops:
  4.6 12.7 %collective-permute-start.10 = (bf16[24,1792]{1,0:T(8,128)(2,1)S(1)}, bf16[24,1792]{1,0:T(8,128)(2,1)S(1)}, u32[]{:S(2)}, u32[]{:S(2)}) collective-permute-start(bf16[24,1792]{1,0:T(8,128)(2,1)S(1)} %get-tuple-element.76), channel_id=1, source_target_pairs={{0,8},{4,12},{8,0},{12,4},{1,9},{5,13},{9,1},{13,5},{2,10},{6,14},... | collective-permute-start | bytes 258056 | tf_op jit(solution)/shard_map/ppermute | solution.py:299
  7.2 10.2 %collective-permute-start.11 = (bf16[24,1792]{1,0:T(8,128)(2,1)S(1)}, bf16[24,1792]{1,0:T(8,128)(2,1)S(1)}, u32[]{:S(2)}, u32[]{:S(2)}) collective-permute-start(bf16[24,1792]{1,0:T(8,128)(2,1)S(1)} %get-tuple-element.77), channel_id=1, source_target_pairs={{0,12},{4,8},{8,4},{12,0},{1,13},{5,9},{9,5},{13,1},{2,14},{6,10},... | collective-permute-start | bytes 258056 | tf_op jit(solution)/shard_map/ppermute | solution.py:299
  7.4 18.6 %collective-permute-start = (bf16[24,1792]{1,0:T(8,128)(2,1)S(1)}, bf16[24,1792]{1,0:T(8,128)(2,1)S(1)}, u32[]{:S(2)}, u32[]{:S(2)}) collective-permute-start(bf16[24,1792]{1,0:T(8,128)(2,1)S(1)} %get-tuple-element.61), channel_id=1, source_target_pairs={{0,4},{4,0},{8,12},{12,8},{1,5},{5,1},{9,13},{13,9},{2,6},{6,2},{1... | collective-permute-start | bytes 258056 | tf_op jit(solution)/shard_map/ppermute | solution.py:299
  8.1 17.9 %collective-permute-start.1 = (bf16[24,1792]{1,0:T(8,128)(2,1)S(1)}, bf16[24,1792]{1,0:T(8,128)(2,1)S(1)}, u32[]{:S(2)}, u32[]{:S(2)}) collective-permute-start(bf16[24,1792]{1,0:T(8,128)(2,1)S(1)} %get-tuple-element.62), channel_id=1, source_target_pairs={{0,8},{4,12},{8,0},{12,4},{1,9},{5,13},{9,1},{13,5},{2,10},{6,14},... | collective-permute-start | bytes 258056 | tf_op jit(solution)/shard_map/ppermute | solution.py:299
  11.6 14.4 %collective-permute-start.2 = (bf16[24,1792]{1,0:T(8,128)(2,1)S(1)}, bf16[24,1792]{1,0:T(8,128)(2,1)S(1)}, u32[]{:S(2)}, u32[]{:S(2)}) collective-permute-start(bf16[24,1792]{1,0:T(8,128)(2,1)S(1)} %get-tuple-element.63), channel_id=1, source_target_pairs={{0,12},{4,8},{8,4},{12,0},{1,13},{5,9},{9,5},{13,1},{2,14},{6,10},... | collective-permute-start | bytes 258056 | tf_op jit(solution)/shard_map/ppermute | solution.py:299
  20.5 9.2 %collective-permute-start.12 = (bf16[112,1024]{1,0:T(8,128)(2,1)S(1)}, bf16[112,1024]{1,0:T(8,128)(2,1)S(1)}, u32[]{:S(2)}, u32[]{:S(2)}) collective-permute-start(bf16[112,1024]{1,0:T(8,128)(2,1)S(1)} %get-tuple-element.79), channel_id=1, source_target_pairs={{0,1},{1,0},{2,3},{3,2},{4,5},{5,4},{6,7},{7,6},{8,9},{9,8},{10,11... | collective-permute-start | bytes 688136 | tf_op jit(solution)/shard_map/ppermute | solution.py:291
  31.4 10.9 %collective-permute-start.4 = (bf16[112,1024]{1,0:T(8,128)(2,1)S(1)}, bf16[112,1024]{1,0:T(8,128)(2,1)S(1)}, u32[]{:S(2)}, u32[]{:S(2)}) collective-permute-start(bf16[112,1024]{1,0:T(8,128)(2,1)S(1)} %shard_map.59.refs_0_), channel_id=1, source_target_pairs={{0,2},{1,3},{2,0},{3,1},{4,6},{5,7},{6,4},{7,5},{8,10},{9,11},{10,... | collective-permute-start | bytes 688136 | tf_op jit(solution)/shard_map/ppermute | solution.py:291
  42.5 16.2 %collective-permute-start.5 = (bf16[96,512]{1,0:T(8,128)(2,1)S(1)}, bf16[96,512]{1,0:T(8,128)(2,1)S(1)}, u32[]{:S(2)}, u32[]{:S(2)}) collective-permute-start(bf16[96,512]{1,0:T(8,128)(2,1)S(1)} %shard_map.60.refs_2_), channel_id=1, source_target_pairs={{0,1},{1,0},{2,3},{3,2},{4,5},{5,4},{6,7},{7,6},{8,9},{9,8},{10,11... | collective-permute-start | bytes 294920 | tf_op jit(solution)/shard_map/ppermute | solution.py:291
  47.3 15.9 %collective-permute-start.15 = (bf16[24,1792]{1,0:T(8,128)(2,1)S(1)}, bf16[24,1792]{1,0:T(8,128)(2,1)S(1)}, u32[]{:S(2)}, u32[]{:S(2)}) collective-permute-start(bf16[24,1792]{1,0:T(8,128)(2,1)S(1)} %get-tuple-element.81), channel_id=1, source_target_pairs={{0,4},{4,0},{8,12},{12,8},{1,5},{5,1},{9,13},{13,9},{2,6},{6,2},{1... | collective-permute-start | bytes 258056 | tf_op jit(solution)/shard_map/ppermute | solution.py:299
  50.3 10.8 %collective-permute-start.18 = (s32[4,2,16]{2,1,0:T(2,128)S(1)}, s32[4,2,16]{2,1,0:T(2,128)S(1)}, u32[]{:S(2)}, u32[]{:S(2)}) collective-permute-start(s32[4,2,16]{2,1,0:T(2,128)S(1)} %bitcast.12), channel_id=1, source_target_pairs={{16,0},{17,1},{18,2},{19,3},{20,4},{21,5},{22,6},{23,7},{24,8},{25... | collective-permute-start | bytes 1544 | tf_op jit(solution)/shard_map/ppermute | solution.py:352
  56.0 10.0 %collective-permute-start.16 = (bf16[24,1792]{1,0:T(8,128)(2,1)S(1)}, bf16[24,1792]{1,0:T(8,128)(2,1)S(1)}, u32[]{:S(2)}, u32[]{:S(2)}) collective-permute-start(bf16[24,1792]{1,0:T(8,128)(2,1)S(1)} %get-tuple-element.82), channel_id=1, source_target_pairs={{0,8},{4,12},{8,0},{12,4},{1,9},{5,13},{9,1},{13,5},{2,10},{6,14},... | collective-permute-start | bytes 258056 | tf_op jit(solution)/shard_map/ppermute | solution.py:299
  61.1 11.3 %collective-permute-start.7 = (bf16[24,1792]{1,0:T(8,128)(2,1)S(1)}, bf16[24,1792]{1,0:T(8,128)(2,1)S(1)}, u32[]{:S(2)}, u32[]{:S(2)}) collective-permute-start(bf16[24,1792]{1,0:T(8,128)(2,1)S(1)} %get-tuple-element.68), channel_id=1, source_target_pairs={{0,8},{4,12},{8,0},{12,4},{1,9},{5,13},{9,1},{13,5},{2,10},{6,14},... | collective-permute-start | bytes 258056 | tf_op jit(solution)/shard_map/ppermute | solution.py:299
  63.2 9.2 %collective-permute-start.8 = (bf16[24,1792]{1,0:T(8,128)(2,1)S(1)}, bf16[24,1792]{1,0:T(8,128)(2,1)S(1)}, u32[]{:S(2)}, u32[]{:S(2)}) collective-permute-start(bf16[24,1792]{1,0:T(8,128)(2,1)S(1)} %get-tuple-element.69), channel_id=1, source_target_pairs={{0,12},{4,8},{8,4},{12,0},{1,13},{5,9},{9,5},{13,1},{2,14},{6,10},... | collective-permute-start | bytes 258056 | tf_op jit(solution)/shard_map/ppermute | solution.py:299
  75.9 13.6 %collective-permute-start.32 = (bf16[24,1792]{1,0:T(8,128)(2,1)S(1)}, bf16[24,1792]{1,0:T(8,128)(2,1)S(1)}, u32[]{:S(2)}, u32[]{:S(2)}) collective-permute-start(bf16[24,1792]{1,0:T(8,128)(2,1)S(1)} %get-tuple-element.97), channel_id=1, source_target_pairs={{0,24},{4,28},{8,16},{12,20},{1,25},{5,29},{9,17},{13,21},{2,26},{... | collective-permute-start | bytes 258056 | tf_op jit(solution)/shard_map/ppermute | solution.py:308
  77.2 13.7 %collective-permute-start.33 = (bf16[24,1792]{1,0:T(8,128)(2,1)S(1)}, bf16[24,1792]{1,0:T(8,128)(2,1)S(1)}, u32[]{:S(2)}, u32[]{:S(2)}) collective-permute-start(bf16[24,1792]{1,0:T(8,128)(2,1)S(1)} %get-tuple-element.98), channel_id=1, source_target_pairs={{0,28},{4,24},{8,20},{12,16},{1,29},{5,25},{9,21},{13,17},{2,30},{... | collective-permute-start | bytes 258056 | tf_op jit(solution)/shard_map/ppermute | solution.py:308
  78.5 15.7 %collective-permute-start.20 = (bf16[24,1792]{1,0:T(8,128)(2,1)S(1)}, bf16[24,1792]{1,0:T(8,128)(2,1)S(1)}, u32[]{:S(2)}, u32[]{:S(2)}) collective-permute-start(bf16[24,1792]{1,0:T(8,128)(2,1)S(1)} %get-tuple-element.85), channel_id=1, source_target_pairs={{0,16},{4,20},{8,24},{12,28},{1,17},{5,21},{9,25},{13,29},{2,18},{... | collective-permute-start | bytes 258056 | tf_op jit(solution)/shard_map/ppermute | solution.py:308
  79.8 14.4 %collective-permute-start.21 = (bf16[24,1792]{1,0:T(8,128)(2,1)S(1)}, bf16[24,1792]{1,0:T(8,128)(2,1)S(1)}, u32[]{:S(2)}, u32[]{:S(2)}) collective-permute-start(bf16[24,1792]{1,0:T(8,128)(2,1)S(1)} %get-tuple-element.86), channel_id=1, source_target_pairs={{0,20},{4,16},{8,28},{12,24},{1,21},{5,17},{9,29},{13,25},{2,22},{... | collective-permute-start | bytes 258056 | tf_op jit(solution)/shard_map/ppermute | solution.py:308
  82.7 13.7 %collective-permute-start.22 = (bf16[24,1792]{1,0:T(8,128)(2,1)S(1)}, bf16[24,1792]{1,0:T(8,128)(2,1)S(1)}, u32[]{:S(2)}, u32[]{:S(2)}) collective-permute-start(bf16[24,1792]{1,0:T(8,128)(2,1)S(1)} %get-tuple-element.87), channel_id=1, source_target_pairs={{0,24},{4,28},{8,16},{12,20},{1,25},{5,29},{9,17},{13,21},{2,26},{... | collective-permute-start | bytes 258056 | tf_op jit(solution)/shard_map/ppermute | solution.py:308
  103.5 11.3 %collective-permute-start.25 = (bf16[112,1024]{1,0:T(8,128)(2,1)S(1)}, bf16[112,1024]{1,0:T(8,128)(2,1)S(1)}, u32[]{:S(2)}, u32[]{:S(2)}) collective-permute-start(bf16[112,1024]{1,0:T(8,128)(2,1)S(1)} %shard_map.70.refs_0_), channel_id=1, source_target_pairs={{0,2},{1,3},{2,0},{3,1},{4,6},{5,7},{6,4},{7,5},{8,10},{9,11},{10,... | collective-permute-start | bytes 688136 | tf_op jit(solution)/shard_map/ppermute | solution.py:291
  104.9 17.8 %collective-permute-start.19 = (bf16[64,1792]{1,0:T(8,128)(2,1)S(1)}, bf16[64,1792]{1,0:T(8,128)(2,1)S(1)}, u32[]{:S(2)}, u32[]{:S(2)}) collective-permute-start(bf16[64,1792]{1,0:T(8,128)(2,1)S(1)} %get-tuple-element.84.kept_ref), channel_id=1, source_target_pairs={{0,16},{1,17},{2,18},{3,19},{4,20},{5,21},{6,22},{7,23},{8,24},{9,... | collective-permute-start | bytes 688136 | tf_op jit(solution)/shard_map/ppermute | solution.py:386
  116.7 10.4 %collective-permute-start.38 = (bf16[24,1792]{1,0:T(8,128)(2,1)S(1)}, bf16[24,1792]{1,0:T(8,128)(2,1)S(1)}, u32[]{:S(2)}, u32[]{:S(2)}) collective-permute-start(bf16[24,1792]{1,0:T(8,128)(2,1)S(1)} %get-tuple-element.103), channel_id=1, source_target_pairs={{0,8},{4,12},{8,0},{12,4},{1,9},{5,13},{9,1},{13,5},{2,10},{6,14},... | collective-permute-start | bytes 258056 | tf_op jit(solution)/shard_map/ppermute | solution.py:299
  117.9 9.2 %collective-permute-start.39 = (bf16[24,1792]{1,0:T(8,128)(2,1)S(1)}, bf16[24,1792]{1,0:T(8,128)(2,1)S(1)}, u32[]{:S(2)}, u32[]{:S(2)}) collective-permute-start(bf16[24,1792]{1,0:T(8,128)(2,1)S(1)} %get-tuple-element.104), channel_id=1, source_target_pairs={{0,12},{4,8},{8,4},{12,0},{1,13},{5,9},{9,5},{13,1},{2,14},{6,10},... | collective-permute-start | bytes 258056 | tf_op jit(solution)/shard_map/ppermute | solution.py:299
  122.7 11.4 %collective-permute-start.28 = (bf16[24,1792]{1,0:T(8,128)(2,1)S(1)}, bf16[24,1792]{1,0:T(8,128)(2,1)S(1)}, u32[]{:S(2)}, u32[]{:S(2)}) collective-permute-start(bf16[24,1792]{1,0:T(8,128)(2,1)S(1)} %get-tuple-element.93), channel_id=1, source_target_pairs={{0,8},{4,12},{8,0},{12,4},{1,9},{5,13},{9,1},{13,5},{2,10},{6,14},... | collective-permute-start | bytes 258056 | tf_op jit(solution)/shard_map/ppermute | solution.py:299
  123.9 10.2 %collective-permute-start.29 = (bf16[24,1792]{1,0:T(8,128)(2,1)S(1)}, bf16[24,1792]{1,0:T(8,128)(2,1)S(1)}, u32[]{:S(2)}, u32[]{:S(2)}) collective-permute-start(bf16[24,1792]{1,0:T(8,128)(2,1)S(1)} %get-tuple-element.94), channel_id=1, source_target_pairs={{0,12},{4,8},{8,4},{12,0},{1,13},{5,9},{9,5},{13,1},{2,14},{6,10},... | collective-permute-start | bytes 258056 | tf_op jit(solution)/shard_map/ppermute | solution.py:299
  (21 other events, 130.4 us)

commit v3 on v2

--- a/solution.py
+++ b/solution.py
@@ -57,6 +57,7 @@
         self.group_pay = peers * self.pay
         self.piece = self.group_pay // self.pieces
         self.all_pay = self.groups * self.group_pay
+        self.all_piece = self.groups * self.piece
         self.each = padded(peers * self.slots, 8)
         self.group_each = self.members * self.each
         self.partial = (self.group_each + EXTRA, 2 * self.half)
@@ -82,8 +83,8 @@
 
 def slot_hits(z, routes_ref):
     row = lax.broadcasted_iota(I32, (z.all_pay, 1), 0)
-    group, rest = divided(row, z.group_pay)
-    step, place = divided(rest, z.pay)
+    step, rest = divided(row, z.groups * z.pay)
+    group, place = divided(rest, z.pay)
     member, inside = divided(place, z.slots)
     batch, rank = divided(inside, CAP)
     rank = jnp.where(member < z.members, rank, -1)
@@ -110,10 +111,30 @@
 def send_rows(z, hits, rows, outs):
     value = dot(hits.astype(BF16), rows)
     for index, out in enumerate(outs):
-        out[...] = value[index * z.piece:(index + 1) * z.piece].astype(BF16)
-
-
-def pack_kernel(z, routes_ref, gates_ref, rows_ref, *outs):
+        out[...] = value[index * z.all_piece:(index + 1) * z.all_piece].astype(BF16)
+
+
+def group_rows(z, group, pieces):
+    result = []
+    for piece in pieces:
+        value = piece[...].astype(F32)
+        for step in range(z.peers // z.pieces):
+            low = (step * z.groups + group) * z.pay
+            result.append(value[low:low + z.pay])
+    return jnp.concatenate(result, axis=0)
+
+
+def pack_kernel(z, *refs):
+    sources, outs = refs[:3], refs[3:-4]
+    routes_ref, gates_ref, rows_ref, sems = refs[-4:]
+    copies = [
+        pltpu.make_async_copy(source, target, sems.at[index])
+        for index, (source, target) in enumerate(zip(sources, refs[-4:-1]))
+    ]
+    for copy in copies:
+        copy.start()
+    for copy in copies:
+        copy.wait()
     hits, first, second = slot_hits(z, routes_ref)
     gates = line_up(z, gates_ref)
     weight = jnp.where(first, gates[0:1, :], F32(0.0)) + jnp.where(second, gates[1:2, :], F32(0.0))
@@ -121,18 +142,18 @@
     send_rows(z, hits, rows_ref[...], outs[:-1])
 
 
-def load_kernel(z, parts, experts, after, gate_up, *refs):
+def load_kernel(z, parts, after, gate_up, *refs):
     outs, sems = refs[:-1], refs[-1]
     flat = gate_up.reshape(2 * z.width, z.units_dev)
     depth = 2 * z.width // parts
     copies = []
-    for index, expert in enumerate(experts):
+    for expert in range(z.local):
         for part in range(parts):
             copies.append(
                 pltpu.make_async_copy(
                     flat.at[pl.ds(part * depth, depth), pl.ds(expert * z.units, z.units)],
-                    outs[index].at[pl.ds(part * depth, depth)],
-                    sems.at[index * parts + part],
+                    outs[expert].at[pl.ds(part * depth, depth)],
+                    sems.at[expert * parts + part],
                 )
             )
     for copy in copies:
@@ -141,16 +162,17 @@
         copy.wait()
 
 
-def load_down_kernel(z, experts, after, down_proj, *refs):
-    outs, sems = refs[:-1], refs[-1]
-    copies = [
-        pltpu.make_async_copy(
-            down_proj.at[0, pl.ds(expert * z.units, z.units), :], outs[index], sems.at[index]
+def load_down_kernel(z, group, after, routes_ref, down_proj, *refs):
+    outs, routes_out, sems = refs[:z.members], refs[z.members], refs[-1]
+    copies = []
+    for index in range(z.members):
+        low = (group * z.members + index) * z.units
+        copies.append(
+            pltpu.make_async_copy(down_proj.at[0, pl.ds(low, z.units), :], outs[index], sems.at[index])
         )
-        for index, expert in enumerate(experts)
-    ]
     for copy in copies:
         copy.start()
+    routes_out[...] = routes_ref[...]
     for copy in copies:
         copy.wait()
 
@@ -164,12 +186,11 @@
     return both
 
 
-def up_kernel(z, *refs):
+def up_kernel(z, group, *refs):
     weights, refs = refs[:z.members], refs[z.members:]
     received, refs = refs[:z.pieces], refs[z.pieces:]
     own, sent, spread, staged = refs
-    stacked = jnp.concatenate([piece[...].astype(F32) for piece in received], axis=0).astype(BF16)
-    rows = dot(z.order(), stacked)
+    rows = dot(z.order(), group_rows(z, group, received).astype(BF16))
     squares = rows * rows
     high = squares.astype(BF16)
     low = (squares - high.astype(F32)).astype(BF16)
@@ -217,9 +238,9 @@
     out[z.group_each:, :] = split_sums(sums, 2 * z.half).astype(BF16)
 
 
-def act_kernel(z, *refs):
+def act_kernel(z, count, *refs):
     out = refs[-1]
-    products, sums = joined(z, refs[:-1])
+    products, sums = joined(z, refs[:count])
     shape = (z.group_each, z.group_each)
     diagonal = lax.broadcasted_iota(I32, shape, 0) == lax.broadcasted_iota(I32, shape, 1)
     sums = jnp.sum(jnp.where(diagonal, sums[:, :z.group_each], F32(0.0)), axis=1, keepdims=True)
@@ -250,7 +271,12 @@
 def combine_kernel(z, tick, last, weight_ref, rows_ref, kept_ref, *refs):
     count = z.groups * z.pieces
     returned, refs = refs[:count], refs[count:]
-    stacked = jnp.concatenate([piece[...].astype(F32) for piece in returned], axis=0).astype(BF16)
+    stacked = []
+    for piece in range(z.pieces):
+        values = [returned[group * z.pieces + piece][...].astype(F32) for group in range(z.groups)]
+        for step in range(z.peers // z.pieces):
+            stacked += [value[step * z.pay:(step + 1) * z.pay] for value in values]
+    stacked = jnp.concatenate(stacked, axis=0).astype(BF16)
     mixed = dot(weight_ref[...], stacked, DOWN)
     value = (rows_ref[...].astype(F32) + mixed).astype(BF16)
     if last:
@@ -282,6 +308,7 @@
     parts = 2 if z.width % 256 == 0 else 1
     shape = jax.ShapeDtypeStruct
     pay = shape((z.piece, z.width), BF16)
+    all_pay = shape((z.all_piece, z.width), BF16)
     whole = shape((z.rows, z.width), BF16)
     steps = sorted(range(z.peers), key=lambda step: -step.bit_length())
     second = 10**6
@@ -308,28 +335,41 @@
             result[step] = lax.ppermute(pieces[step], ("section", "expert"), pairs)
         return result
 
-    def grouped(pieces):
-        return [pieces[group * z.pieces:(group + 1) * z.pieces] for group in range(z.groups)]
-
-    def middle(received, wide):
+    def load_down(group, after):
+        *tall, handed = call(
+            load_down_kernel, (z, group), 1, (0, 2 * second * 3),
+            [pltpu.VMEM((z.units, z.width), BF16)] * z.members + [shape(routes.shape, routes.dtype)],
+            [VMEM, VMEM, HBM], [pltpu.SemaphoreType.DMA((z.members,))],
+            after, routes, down_proj,
+        )
+        return tall, handed
+
+    def middle(received, group, tick):
         own, sent = call(
-            up_kernel, (z,), 6, (0, 3 * second * 3),
+            up_kernel, (z, group), 6, (0, 3 * second * 3),
             [shape(z.partial, F32), shape(z.partial, BF16)],
             [VMEM] * (z.members + z.pieces),
             [
                 pltpu.VMEM((z.members, 2 * z.each, 2 * z.width), BF16),
                 pltpu.VMEM((2,) + z.partial, F32),
             ],
-            *wide, *received,
+            *wide[group * z.members:(group + 1) * z.members], *received,
         )
         pair = call(
             pair_kernel, (z,), 2, (0, second), [shape(z.partial, BF16)], [VMEM] * 2, [],
             own, swap(sent, 1),
         )[0]
         pairs = [pair] + [swap(pair, step) for step in range(2, z.splits, 2)]
+        if tick == 0:
+            tall[group], handed = load_down(group, pair)
+            if group == 0:
+                pairs_back = [(i + 1, i) for i in range(sections - 1)]
+                following.append(lax.ppermute(handed, "section", pairs_back))
+        waits = tall[group][:1] + following[:group] if tick == 0 else []
         units = call(
-            act_kernel, (z,), 2, (0, second),
-            [shape((z.group_each, z.half), BF16)], [VMEM] * len(pairs), [], *pairs,
+            act_kernel, (z, len(pairs)), 2, (0, second),
+            [shape((z.group_each, z.half), BF16)], [VMEM] * (len(pairs) + len(waits)), [],
+            *pairs, *waits,
         )[0]
         return units, swap(units, 1)
 
@@ -345,44 +385,40 @@
     kept = rows
     *sent, weight = call(
         pack_kernel, (z,), 3, (0, second),
-        [pay] * (z.groups * z.pieces) + [shape((z.all_pay, z.rows), BF16)],
-        [VMEM] * 3, [], routes, gates, rows,
+        [all_pay] * z.pieces + [shape((z.all_pay, z.rows), BF16)],
+        [HBM] * 3,
+        [
+            pltpu.VMEM(routes.shape, routes.dtype),
+            pltpu.VMEM(gates.shape, gates.dtype),
+            pltpu.VMEM(rows.shape, rows.dtype),
+            pltpu.SemaphoreType.DMA((3,)),
+        ],
+        *(pltpu.with_memory_space_constraint(value, pltpu.HBM) for value in (routes, gates, rows)),
     )
-    received = [exchanged(pieces) for pieces in grouped(sent)]
-    following = lax.ppermute(routes, "section", [(i + 1, i) for i in range(sections - 1)])
+    received = exchanged(sent)
     gate_up = pltpu.with_memory_space_constraint(gate_up, pltpu.HBM)
     down_proj = pltpu.with_memory_space_constraint(down_proj, pltpu.HBM)
-    wide, tall = [], []
-    for group in range(z.groups):
-        experts = range(group * z.members, (group + 1) * z.members)
-        wide.append(call(
-            load_kernel, (z, parts, experts), 1, (0, 5 * second * 3),
-            [pltpu.VMEM((2 * z.width, z.units), BF16)] * z.members, [VMEM, HBM],
-            [pltpu.SemaphoreType.DMA((z.members * parts,))],
-            weight, gate_up,
-        ))
-    for group in range(z.groups):
-        experts = range(group * z.members, (group + 1) * z.members)
-        tall.append(call(
-            load_down_kernel, (z, experts), 1, (0, 2 * second * 3),
-            [pltpu.VMEM((z.units, z.width), BF16)] * z.members, [VMEM, HBM],
-            [pltpu.SemaphoreType.DMA((z.members,))],
-            weight, down_proj,
-        ))
+    wide = call(
+        load_kernel, (z, parts), 1, (0, 10 * second * 3),
+        [pltpu.VMEM((2 * z.width, z.units), BF16)] * z.local, [VMEM, HBM],
+        [pltpu.SemaphoreType.DMA((z.local * parts,))],
+        weight, gate_up,
+    )
+    tall, following = {}, []
     for tick in range(sections):
-        halves = [middle(received[group], wide[group]) for group in range(z.groups)]
+        halves = [middle(received, group, tick) for group in range(z.groups)]
         returned = []
         for group in range(z.groups):
             returned += exchanged(after(halves[group], tall[group]))
         last = tick == sections - 1
         kept, *sent = call(
             combine_kernel, (z, tick, last), 4, (0, second),
-            [whole] if last else [whole] + [pay] * (z.groups * z.pieces),
+            [whole] if last else [whole] + [all_pay] * z.pieces,
             [VMEM] * (3 + len(returned) + (not last)), [],
-            weight, rows, kept, *returned, *([] if last else [following]),
+            weight, rows, kept, *returned, *([] if last else following),
         )
         if not last:
-            received = [relayed(pieces, tick) for pieces in grouped(sent)]
+            received = relayed(sent, tick)
             rows = lax.ppermute(kept, "section", [(tick, tick + 1)])
     return kept.reshape(1, z.micro, z.tok, z.width)
 

time: 136 us -> 128 us (0.941)
  starting transfers between devices: 49 us -> 40.3 us
  waiting for transfers between devices: 44.1 us -> 47.5 us
  local copies, waits for them, and re-layouts: 2.32 us -> 0.01 us
    ppermute x12, waiting for transfers between devices: 17.9 us -> 10.9 us  [swap(): return lax.ppermute(value, 'hidden', pairs)]
    ppermute x18 -> x15, waiting for transfers between devices: 14.8 us -> 20.7 us  [exchanged(): result[step] = lax.ppermute(pieces[step], 'expert', pairs)]
    ppermute x8 -> x4, starting transfers between devices: 10.5 us -> 5.35 us  [relayed(): result[step] = lax.ppermute(pieces[step], ('section', 'expert'), pairs)]
    ppermute x8 -> x4, waiting for transfers between devices: 11.4 us -> 15.9 us  [relayed(): result[step] = lax.ppermute(pieces[step], ('section', 'expert'), pairs)]
    ppermute x18 -> x15, starting transfers between devices: 28.1 us -> 24.2 us  [exchanged(): result[step] = lax.ppermute(pieces[step], 'expert', pairs)]
    unnamed x10 -> x4, local copies, waits for them, and re-layouts: 2.32 us -> 0.01 us
    pallas_call x23 -> x22, Pallas kernels: 39.2 us -> 39.8 us  [call(): pl.pallas_call(functools.partial(kernel, *sizes), out_shape=outs, in_spec...]
  transfers between devices with their start and end apart: 40 -> 33, of which waited for: 13 -> 12; matrix products, arithmetic and copies ran while one was open for 0% -> 0% of each run, Pallas kernels for 27% -> 23%
where the time goes in v3:
time: 128 us
  waiting for transfers between devices  47.5 us (37%)
  starting transfers between devices  40.3 us (31%)
  Pallas kernels  39.8 us (31%)
    pallas_call x22, Pallas kernels, call(): pl.pallas_call(functools.partial(kernel, *sizes), out_shape=outs, in_spec...  39.8 us
    ppermute x15, starting transfers between devices, exchanged(): result[step] = lax.ppermute(pieces[step], 'expert', pairs)  24.2 us
    ppermute x15, waiting for transfers between devices, exchanged(): result[step] = lax.ppermute(pieces[step], 'expert', pairs)  20.7 us
    ppermute x4, waiting for transfers between devices, relayed(): result[step] = lax.ppermute(pieces[step], ('section', 'expert'), pairs)  15.9 us
    ppermute x12, waiting for transfers between devices, swap(): return lax.ppermute(value, 'hidden', pairs)  10.9 us
    ppermute x12, starting transfers between devices, swap(): return lax.ppermute(value, 'hidden', pairs)  7.06 us
    ppermute x4, starting transfers between devices, relayed(): result[step] = lax.ppermute(pieces[step], ('section', 'expert'), pairs)  5.35 us
  transfers between devices with their start and end apart: 33, of which 12 were waited for; matrix products, arithmetic and copies ran while one was open for 0% of the time, Pallas kernels for 23%

profile of v3, /device:TPU:2, one launch (start us, length us, event | category | flops | bytes accessed | tf_op | source)
XLA Modules:
  0.0 127.9 jit_solution(4072904171248875653)
XLA Ops:
  0.0 1.6 %shard_map.55 = (bf16[48,1792]{1,0:T(8,128)(2,1)S(1)}, bf16[48,1792]{1,0:T(8,128)(2,1)S(1)}, bf16[48,1792]{1,0:T(8,128)(2,1)S(1)}, bf16[48,1792]{1,0:T(8,128)(2,1)S(1)}, bf16[192,64]{1,0:T(8,128)(2,1)S(1)}) custom-call(s32[4,2,16]{2,1,0:T(2,128)} %bitcast.11, bf16[4,2,16]{2,1,0:T(2,128)(2,1)} %bitcast.14, bf16[64,1792]{1,0:T(8,128)(2,1)} %bitcast.8), custom_call_target="tpu_custom_call" | custom-call | bytes 1000000 | tf_op jit(solution)/shard_map/pallas_call | solution.py:293
  1.6 1.6 %collective-permute-start = (bf16[48,1792]{1,0:T(8,128)(2,1)S(1)}, bf16[48,1792]{1,0:T(8,128)(2,1)S(1)}, u32[]{:S(2)}, u32[]{:S(2)}) collective-permute-start(bf16[48,1792]{1,0:T(8,128)(2,1)S(1)} %get-tuple-element.52), channel_id=1, source_target_pairs={{0,4},{4,0},{8,12},{12,8},{1,5},{5,1},{9,13},{13,9},{2,6},{6,2},{1... | collective-permute-start | bytes 516104 | tf_op jit(solution)/shard_map/ppermute | solution.py:326
  3.3 2.6 %collective-permute-start.1 = (bf16[48,1792]{1,0:T(8,128)(2,1)S(1)}, bf16[48,1792]{1,0:T(8,128)(2,1)S(1)}, u32[]{:S(2)}, u32[]{:S(2)}) collective-permute-start(bf16[48,1792]{1,0:T(8,128)(2,1)S(1)} %get-tuple-element.53), channel_id=1, source_target_pairs={{0,8},{4,12},{8,0},{12,4},{1,9},{5,13},{9,1},{13,5},{2,10},{6,14},... | collective-permute-start | bytes 516104 | tf_op jit(solution)/shard_map/ppermute | solution.py:326
  6.1 9.6 %shard_map.56 = (bf16[3584,1024]{1,0:T(8,128)(2,1)S(1)}, bf16[3584,1024]{1,0:T(8,128)(2,1)S(1)}, bf16[3584,1024]{1,0:T(8,128)(2,1)S(1)}, bf16[3584,1024]{1,0:T(8,128)(2,1)S(1)}) custom-call(bf16[192,64]{1,0:T(8,128)(2,1)S(1)} %get-tuple-element.48.after.weight_ref, bf16[1,1792,2,4096]{3,2,1,0:T(2,128)(2,1)} %gate_up.1), custom_call_target="tpu_custom_call" | custom-call | bytes 30000000 | tf_op jit(solution)/shard_map/pallas_call | solution.py:293
  15.8 3.1 %collective-permute-done.1.refs_4_ = bf16[48,1792]{1,0:T(8,128)(2,1)S(1)} collective-permute-done((bf16[48,1792]{1,0:T(8,128)(2,1)S(1)}, bf16[48,1792]{1,0:T(8,128)(2,1)S(1)}, u32[]{:S(2)}, u32[]{:S(2)}) %collective-permute-start.1) | collective-permute-done | bytes 172064 | tf_op jit(solution)/shard_map/ppermute | solution.py:326
  18.9 3.2 %shard_map.57 = (f32[112,1024]{1,0:T(8,128)S(1)}, bf16[112,1024]{1,0:T(8,128)(2,1)S(1)}) custom-call(bf16[3584,1024]{1,0:T(8,128)(2,1)S(1)} %get-tuple-element.49.refs_0_, bf16[3584,1024]{1,0:T(8,128)(2,1)S(1)} %get-tuple-element.50.refs_1_, bf16[48,1792]{1,0:T(8,128)(2,1)S(1)} %get-tuple-element.51.refs_2_, ...), custom_call_target="tpu_custom_call" | custom-call | bytes 9000000 | tf_op jit(solution)/shard_map/pallas_call | solution.py:293
  22.1 3.2 %shard_map.62 = (f32[112,1024]{1,0:T(8,128)S(1)}, bf16[112,1024]{1,0:T(8,128)(2,1)S(1)}) custom-call(bf16[3584,1024]{1,0:T(8,128)(2,1)S(1)} %get-tuple-element.63.refs_0_, bf16[3584,1024]{1,0:T(8,128)(2,1)S(1)} %get-tuple-element.64.refs_1_, bf16[48,1792]{1,0:T(8,128)(2,1)S(1)} %get-tuple-element.51.refs_2_, ...), custom_call_target="tpu_custom_call" | custom-call | bytes 9000000 | tf_op jit(solution)/shard_map/pallas_call | solution.py:293
  28.6 3.2 %shard_map.59 = (bf16[1024,1792]{1,0:T(8,128)(2,1)S(1)}, bf16[1024,1792]{1,0:T(8,128)(2,1)S(1)}, s32[4,2,16]{2,1,0:T(2,128)S(1)}) custom-call(bf16[112,1024]{1,0:T(8,128)(2,1)S(1)} %shard_map.58.after.refs_0_, s32[4,2,16]{2,1,0:T(2,128)S(1)} %bitcast.12, bf16[1,4096,1792]{2,1,0:T(8,128)(2,1)} %down_proj.3), custom_call_target="tpu_custom_call" | custom-call | bytes 6000000 | tf_op jit(solution)/shard_map/pallas_call | solution.py:293
  31.8 2.6 %collective-permute-done.4.refs_1_ = bf16[112,1024]{1,0:T(8,128)(2,1)S(1)} collective-permute-done((bf16[112,1024]{1,0:T(8,128)(2,1)S(1)}, bf16[112,1024]{1,0:T(8,128)(2,1)S(1)}, u32[]{:S(2)}, u32[]{:S(2)}) %collective-permute-start.4) | collective-permute-done | bytes 229408 | tf_op jit(solution)/shard_map/ppermute | solution.py:318
  34.7 2.4 %collective-permute-start.11 = (s32[4,2,16]{2,1,0:T(2,128)S(1)}, s32[4,2,16]{2,1,0:T(2,128)S(1)}, u32[]{:S(2)}, u32[]{:S(2)}) collective-permute-start(s32[4,2,16]{2,1,0:T(2,128)S(1)} %get-tuple-element.69), channel_id=1, source_target_pairs={{16,0},{17,1},{18,2},{19,3},{20,4},{21,5},{22,6},{23,7},{24,8},{25... | collective-permute-start | bytes 1544 | tf_op jit(solution)/shard_map/ppermute | solution.py:367
  37.2 3.8 %shard_map.64 = (bf16[1024,1792]{1,0:T(8,128)(2,1)S(1)}, bf16[1024,1792]{1,0:T(8,128)(2,1)S(1)}, s32[4,2,16]{2,1,0:T(2,128)}) custom-call(bf16[112,1024]{1,0:T(8,128)(2,1)S(1)} %shard_map.63.after.refs_0_, s32[4,2,16]{2,1,0:T(2,128)S(1)} %bitcast.13, bf16[1,4096,1792]{2,1,0:T(8,128)(2,1)} %down_proj.3), custom_call_target="tpu_custom_call" | custom-call | bytes 6000000 | tf_op jit(solution)/shard_map/pallas_call | solution.py:293
  43.0 2.9 %collective-permute-start.6 = (bf16[24,1792]{1,0:T(8,128)(2,1)S(1)}, bf16[24,1792]{1,0:T(8,128)(2,1)S(1)}, u32[]{:S(2)}, u32[]{:S(2)}) collective-permute-start(bf16[24,1792]{1,0:T(8,128)(2,1)S(1)} %get-tuple-element.60), channel_id=1, source_target_pairs={{0,4},{4,0},{8,12},{12,8},{1,5},{5,1},{9,13},{13,9},{2,6},{6,2},{1... | collective-permute-start | bytes 258056 | tf_op jit(solution)/shard_map/ppermute | solution.py:326
  51.0 2.0 %collective-permute-start.14 = (bf16[24,1792]{1,0:T(8,128)(2,1)S(1)}, bf16[24,1792]{1,0:T(8,128)(2,1)S(1)}, u32[]{:S(2)}, u32[]{:S(2)}) collective-permute-start(bf16[24,1792]{1,0:T(8,128)(2,1)S(1)} %get-tuple-element.72), channel_id=1, source_target_pairs={{0,8},{4,12},{8,0},{12,4},{1,9},{5,13},{9,1},{13,5},{2,10},{6,14},... | collective-permute-start | bytes 258056 | tf_op jit(solution)/shard_map/ppermute | solution.py:326
  56.4 6.6 %collective-permute-done.14.refs_6_ = bf16[24,1792]{1,0:T(8,128)(2,1)S(1)} collective-permute-done((bf16[24,1792]{1,0:T(8,128)(2,1)S(1)}, bf16[24,1792]{1,0:T(8,128)(2,1)S(1)}, u32[]{:S(2)}, u32[]{:S(2)}) %collective-permute-start.14) | collective-permute-done | bytes 86048 | tf_op jit(solution)/shard_map/ppermute | solution.py:326
  69.2 8.5 %collective-permute-done.17.refs_2_ = bf16[48,1792]{1,0:T(8,128)(2,1)S(1)} collective-permute-done((bf16[48,1792]{1,0:T(8,128)(2,1)S(1)}, bf16[48,1792]{1,0:T(8,128)(2,1)S(1)}, u32[]{:S(2)}, u32[]{:S(2)}) %collective-permute-start.17) | collective-permute-done | bytes 172064 | tf_op jit(solution)/shard_map/ppermute | solution.py:335
  77.6 7.4 %collective-permute-done.19.refs_4_ = bf16[48,1792]{1,0:T(8,128)(2,1)S(1)} collective-permute-done((bf16[48,1792]{1,0:T(8,128)(2,1)S(1)}, bf16[48,1792]{1,0:T(8,128)(2,1)S(1)}, u32[]{:S(2)}, u32[]{:S(2)}) %collective-permute-start.19) | collective-permute-done | bytes 172064 | tf_op jit(solution)/shard_map/ppermute | solution.py:335
  85.1 3.2 %shard_map.72 = (f32[112,1024]{1,0:T(8,128)S(1)}, bf16[112,1024]{1,0:T(8,128)(2,1)S(1)}) custom-call(bf16[3584,1024]{1,0:T(8,128)(2,1)S(1)} %get-tuple-element.63.refs_0_, bf16[3584,1024]{1,0:T(8,128)(2,1)S(1)} %get-tuple-element.64.refs_1_, bf16[48,1792]{1,0:T(8,128)(2,1)S(1)} %collective-permute-done.17.refs_2_, ...), custom_call_target="tpu_custom_call" | custom-call | bytes 9000000 | tf_op jit(solution)/shard_map/pallas_call | solution.py:293
  88.3 3.2 %shard_map.68 = (f32[112,1024]{1,0:T(8,128)S(1)}, bf16[112,1024]{1,0:T(8,128)(2,1)S(1)}) custom-call(bf16[3584,1024]{1,0:T(8,128)(2,1)S(1)} %get-tuple-element.49.refs_0_, bf16[3584,1024]{1,0:T(8,128)(2,1)S(1)} %get-tuple-element.50.refs_1_, bf16[48,1792]{1,0:T(8,128)(2,1)S(1)} %collective-permute-done.17.refs_2_, ...), custom_call_target="tpu_custom_call" | custom-call | bytes 9000000 | tf_op jit(solution)/shard_map/pallas_call | solution.py:293
  96.2 4.5 %collective-permute-done.28.refs_1_ = bf16[112,1024]{1,0:T(8,128)(2,1)S(1)} collective-permute-done((bf16[112,1024]{1,0:T(8,128)(2,1)S(1)}, bf16[112,1024]{1,0:T(8,128)(2,1)S(1)}, u32[]{:S(2)}, u32[]{:S(2)}) %collective-permute-start.28) | collective-permute-done | bytes 229408 | tf_op jit(solution)/shard_map/ppermute | solution.py:318
  100.9 3.7 %collective-permute-done.22.refs_1_ = bf16[112,1024]{1,0:T(8,128)(2,1)S(1)} collective-permute-done((bf16[112,1024]{1,0:T(8,128)(2,1)S(1)}, bf16[112,1024]{1,0:T(8,128)(2,1)S(1)}, u32[]{:S(2)}, u32[]{:S(2)}) %collective-permute-start.22) | collective-permute-done | bytes 229408 | tf_op jit(solution)/shard_map/ppermute | solution.py:318
  106.5 3.0 %collective-permute-start.30 = (bf16[24,1792]{1,0:T(8,128)(2,1)S(1)}, bf16[24,1792]{1,0:T(8,128)(2,1)S(1)}, u32[]{:S(2)}, u32[]{:S(2)}) collective-permute-start(bf16[24,1792]{1,0:T(8,128)(2,1)S(1)} %get-tuple-element.88), channel_id=1, source_target_pairs={{0,4},{4,0},{8,12},{12,8},{1,5},{5,1},{9,13},{13,9},{2,6},{6,2},{1... | collective-permute-start | bytes 258056 | tf_op jit(solution)/shard_map/ppermute | solution.py:326
  110.3 1.6 %collective-permute-start.32 = (bf16[24,1792]{1,0:T(8,128)(2,1)S(1)}, bf16[24,1792]{1,0:T(8,128)(2,1)S(1)}, u32[]{:S(2)}, u32[]{:S(2)}) collective-permute-start(bf16[24,1792]{1,0:T(8,128)(2,1)S(1)} %get-tuple-element.90), channel_id=1, source_target_pairs={{0,12},{4,8},{8,4},{12,0},{1,13},{5,9},{9,5},{13,1},{2,14},{6,10},... | collective-permute-start | bytes 258056 | tf_op jit(solution)/shard_map/ppermute | solution.py:326
  114.6 1.7 %collective-permute-start.25 = (bf16[24,1792]{1,0:T(8,128)(2,1)S(1)}, bf16[24,1792]{1,0:T(8,128)(2,1)S(1)}, u32[]{:S(2)}, u32[]{:S(2)}) collective-permute-start(bf16[24,1792]{1,0:T(8,128)(2,1)S(1)} %get-tuple-element.83), channel_id=1, source_target_pairs={{0,8},{4,12},{8,0},{12,4},{1,9},{5,13},{9,1},{13,5},{2,10},{6,14},... | collective-permute-start | bytes 258056 | tf_op jit(solution)/shard_map/ppermute | solution.py:326
  120.4 6.5 %collective-permute-done.25.refs_2_ = bf16[24,1792]{1,0:T(8,128)(2,1)S(1)} collective-permute-done((bf16[24,1792]{1,0:T(8,128)(2,1)S(1)}, bf16[24,1792]{1,0:T(8,128)(2,1)S(1)}, u32[]{:S(2)}, u32[]{:S(2)}) %collective-permute-start.25) | collective-permute-done | bytes 86048 | tf_op jit(solution)/shard_map/ppermute | solution.py:326
  (68 shorter events, 35.8 us)
Async XLA Ops:
  1.6 14.1 %collective-permute-start = (bf16[48,1792]{1,0:T(8,128)(2,1)S(1)}, bf16[48,1792]{1,0:T(8,128)(2,1)S(1)}, u32[]{:S(2)}, u32[]{:S(2)}) collective-permute-start(bf16[48,1792]{1,0:T(8,128)(2,1)S(1)} %get-tuple-element.52), channel_id=1, source_target_pairs={{0,4},{4,0},{8,12},{12,8},{1,5},{5,1},{9,13},{13,9},{2,6},{6,2},{1... | collective-permute-start | bytes 516104 | tf_op jit(solution)/shard_map/ppermute | solution.py:326
  3.3 15.6 %collective-permute-start.1 = (bf16[48,1792]{1,0:T(8,128)(2,1)S(1)}, bf16[48,1792]{1,0:T(8,128)(2,1)S(1)}, u32[]{:S(2)}, u32[]{:S(2)}) collective-permute-start(bf16[48,1792]{1,0:T(8,128)(2,1)S(1)} %get-tuple-element.53), channel_id=1, source_target_pairs={{0,8},{4,12},{8,0},{12,4},{1,9},{5,13},{9,1},{13,5},{2,10},{6,14},... | collective-permute-start | bytes 516104 | tf_op jit(solution)/shard_map/ppermute | solution.py:326
  5.9 13.0 %collective-permute-start.2 = (bf16[48,1792]{1,0:T(8,128)(2,1)S(1)}, bf16[48,1792]{1,0:T(8,128)(2,1)S(1)}, u32[]{:S(2)}, u32[]{:S(2)}) collective-permute-start(bf16[48,1792]{1,0:T(8,128)(2,1)S(1)} %get-tuple-element.54), channel_id=1, source_target_pairs={{0,12},{4,8},{8,4},{12,0},{1,13},{5,9},{9,5},{13,1},{2,14},{6,10},... | collective-permute-start | bytes 516104 | tf_op jit(solution)/shard_map/ppermute | solution.py:326
  25.9 8.5 %collective-permute-start.4 = (bf16[112,1024]{1,0:T(8,128)(2,1)S(1)}, bf16[112,1024]{1,0:T(8,128)(2,1)S(1)}, u32[]{:S(2)}, u32[]{:S(2)}) collective-permute-start(bf16[112,1024]{1,0:T(8,128)(2,1)S(1)} %shard_map.58.after.refs_0_), channel_id=1, source_target_pairs={{0,2},{1,3},{2,0},{3,1},{4,6},{5,7},{6,4},{7,5},{8,10},{9,11},{10,... | collective-permute-start | bytes 688136 | tf_op jit(solution)/shard_map/ppermute | solution.py:318
  27.6 13.4 %collective-permute-start.10 = (bf16[112,1024]{1,0:T(8,128)(2,1)S(1)}, bf16[112,1024]{1,0:T(8,128)(2,1)S(1)}, u32[]{:S(2)}, u32[]{:S(2)}) collective-permute-start(bf16[112,1024]{1,0:T(8,128)(2,1)S(1)} %shard_map.63.after.refs_0_), channel_id=1, source_target_pairs={{0,2},{1,3},{2,0},{3,1},{4,6},{5,7},{6,4},{7,5},{8,10},{9,11},{10,... | collective-permute-start | bytes 688136 | tf_op jit(solution)/shard_map/ppermute | solution.py:318
  41.1 7.2 %collective-permute-start.12 = (bf16[96,512]{1,0:T(8,128)(2,1)S(1)}, bf16[96,512]{1,0:T(8,128)(2,1)S(1)}, u32[]{:S(2)}, u32[]{:S(2)}) collective-permute-start(bf16[96,512]{1,0:T(8,128)(2,1)S(1)} %shard_map.65.refs_2_), channel_id=1, source_target_pairs={{0,1},{1,0},{2,3},{3,2},{4,5},{5,4},{6,7},{7,6},{8,9},{9,8},{10,11... | collective-permute-start | bytes 294920 | tf_op jit(solution)/shard_map/ppermute | solution.py:318
  43.0 10.0 %collective-permute-start.6 = (bf16[24,1792]{1,0:T(8,128)(2,1)S(1)}, bf16[24,1792]{1,0:T(8,128)(2,1)S(1)}, u32[]{:S(2)}, u32[]{:S(2)}) collective-permute-start(bf16[24,1792]{1,0:T(8,128)(2,1)S(1)} %get-tuple-element.60), channel_id=1, source_target_pairs={{0,4},{4,0},{8,12},{12,8},{1,5},{5,1},{9,13},{13,9},{2,6},{6,2},{1... | collective-permute-start | bytes 258056 | tf_op jit(solution)/shard_map/ppermute | solution.py:326
  45.9 9.8 %collective-permute-start.7 = (bf16[24,1792]{1,0:T(8,128)(2,1)S(1)}, bf16[24,1792]{1,0:T(8,128)(2,1)S(1)}, u32[]{:S(2)}, u32[]{:S(2)}) collective-permute-start(bf16[24,1792]{1,0:T(8,128)(2,1)S(1)} %get-tuple-element.61), channel_id=1, source_target_pairs={{0,8},{4,12},{8,0},{12,4},{1,9},{5,13},{9,1},{13,5},{2,10},{6,14},... | collective-permute-start | bytes 258056 | tf_op jit(solution)/shard_map/ppermute | solution.py:326
  46.9 8.7 %collective-permute-start.8 = (bf16[24,1792]{1,0:T(8,128)(2,1)S(1)}, bf16[24,1792]{1,0:T(8,128)(2,1)S(1)}, u32[]{:S(2)}, u32[]{:S(2)}) collective-permute-start(bf16[24,1792]{1,0:T(8,128)(2,1)S(1)} %get-tuple-element.62), channel_id=1, source_target_pairs={{0,12},{4,8},{8,4},{12,0},{1,13},{5,9},{9,5},{13,1},{2,14},{6,10},... | collective-permute-start | bytes 258056 | tf_op jit(solution)/shard_map/ppermute | solution.py:326
  51.0 12.0 %collective-permute-start.14 = (bf16[24,1792]{1,0:T(8,128)(2,1)S(1)}, bf16[24,1792]{1,0:T(8,128)(2,1)S(1)}, u32[]{:S(2)}, u32[]{:S(2)}) collective-permute-start(bf16[24,1792]{1,0:T(8,128)(2,1)S(1)} %get-tuple-element.72), channel_id=1, source_target_pairs={{0,8},{4,12},{8,0},{12,4},{1,9},{5,13},{9,1},{13,5},{2,10},{6,14},... | collective-permute-start | bytes 258056 | tf_op jit(solution)/shard_map/ppermute | solution.py:326
  53.0 10.1 %collective-permute-start.15 = (bf16[24,1792]{1,0:T(8,128)(2,1)S(1)}, bf16[24,1792]{1,0:T(8,128)(2,1)S(1)}, u32[]{:S(2)}, u32[]{:S(2)}) collective-permute-start(bf16[24,1792]{1,0:T(8,128)(2,1)S(1)} %get-tuple-element.73), channel_id=1, source_target_pairs={{0,12},{4,8},{8,4},{12,0},{1,13},{5,9},{9,5},{13,1},{2,14},{6,10},... | collective-permute-start | bytes 258056 | tf_op jit(solution)/shard_map/ppermute | solution.py:326
  63.8 13.9 %collective-permute-start.17 = (bf16[48,1792]{1,0:T(8,128)(2,1)S(1)}, bf16[48,1792]{1,0:T(8,128)(2,1)S(1)}, u32[]{:S(2)}, u32[]{:S(2)}) collective-permute-start(bf16[48,1792]{1,0:T(8,128)(2,1)S(1)} %get-tuple-element.75), channel_id=1, source_target_pairs={{0,16},{4,20},{8,24},{12,28},{1,17},{5,21},{9,25},{13,29},{2,18},{... | collective-permute-start | bytes 516104 | tf_op jit(solution)/shard_map/ppermute | solution.py:335
  65.1 12.6 %collective-permute-start.18 = (bf16[48,1792]{1,0:T(8,128)(2,1)S(1)}, bf16[48,1792]{1,0:T(8,128)(2,1)S(1)}, u32[]{:S(2)}, u32[]{:S(2)}) collective-permute-start(bf16[48,1792]{1,0:T(8,128)(2,1)S(1)} %get-tuple-element.76), channel_id=1, source_target_pairs={{0,20},{4,16},{8,28},{12,24},{1,21},{5,17},{9,29},{13,25},{2,22},{... | collective-permute-start | bytes 516104 | tf_op jit(solution)/shard_map/ppermute | solution.py:335
  66.4 18.7 %collective-permute-start.19 = (bf16[48,1792]{1,0:T(8,128)(2,1)S(1)}, bf16[48,1792]{1,0:T(8,128)(2,1)S(1)}, u32[]{:S(2)}, u32[]{:S(2)}) collective-permute-start(bf16[48,1792]{1,0:T(8,128)(2,1)S(1)} %get-tuple-element.77), channel_id=1, source_target_pairs={{0,24},{4,28},{8,16},{12,20},{1,25},{5,29},{9,17},{13,21},{2,26},{... | collective-permute-start | bytes 516104 | tf_op jit(solution)/shard_map/ppermute | solution.py:335
  67.7 17.4 %collective-permute-start.20 = (bf16[48,1792]{1,0:T(8,128)(2,1)S(1)}, bf16[48,1792]{1,0:T(8,128)(2,1)S(1)}, u32[]{:S(2)}, u32[]{:S(2)}) collective-permute-start(bf16[48,1792]{1,0:T(8,128)(2,1)S(1)} %get-tuple-element.78), channel_id=1, source_target_pairs={{0,28},{4,24},{8,20},{12,16},{1,29},{5,25},{9,21},{13,17},{2,30},{... | collective-permute-start | bytes 516104 | tf_op jit(solution)/shard_map/ppermute | solution.py:335
  92.1 8.5 %collective-permute-start.28 = (bf16[112,1024]{1,0:T(8,128)(2,1)S(1)}, bf16[112,1024]{1,0:T(8,128)(2,1)S(1)}, u32[]{:S(2)}, u32[]{:S(2)}) collective-permute-start(bf16[112,1024]{1,0:T(8,128)(2,1)S(1)} %shard_map.73.refs_0_), channel_id=1, source_target_pairs={{0,2},{1,3},{2,0},{3,1},{4,6},{5,7},{6,4},{7,5},{8,10},{9,11},{10,... | collective-permute-start | bytes 688136 | tf_op jit(solution)/shard_map/ppermute | solution.py:318
  93.8 10.9 %collective-permute-start.22 = (bf16[112,1024]{1,0:T(8,128)(2,1)S(1)}, bf16[112,1024]{1,0:T(8,128)(2,1)S(1)}, u32[]{:S(2)}, u32[]{:S(2)}) collective-permute-start(bf16[112,1024]{1,0:T(8,128)(2,1)S(1)} %shard_map.69.refs_0_), channel_id=1, source_target_pairs={{0,2},{1,3},{2,0},{3,1},{4,6},{5,7},{6,4},{7,5},{8,10},{9,11},{10,... | collective-permute-start | bytes 688136 | tf_op jit(solution)/shard_map/ppermute | solution.py:318
  94.9 19.7 %collective-permute-start.16 = (bf16[64,1792]{1,0:T(8,128)(2,1)S(1)}, bf16[64,1792]{1,0:T(8,128)(2,1)S(1)}, u32[]{:S(2)}, u32[]{:S(2)}) collective-permute-start(bf16[64,1792]{1,0:T(8,128)(2,1)S(1)} %get-tuple-element.74.kept_ref), channel_id=1, source_target_pairs={{0,16},{1,17},{2,18},{3,19},{4,20},{5,21},{6,22},{7,23},{8,24},{9,... | collective-permute-start | bytes 688136 | tf_op jit(solution)/shard_map/ppermute | solution.py:422
  104.8 7.1 %collective-permute-start.23 = (bf16[96,512]{1,0:T(8,128)(2,1)S(1)}, bf16[96,512]{1,0:T(8,128)(2,1)S(1)}, u32[]{:S(2)}, u32[]{:S(2)}) collective-permute-start(bf16[96,512]{1,0:T(8,128)(2,1)S(1)} %shard_map.70.refs_2_), channel_id=1, source_target_pairs={{0,1},{1,0},{2,3},{3,2},{4,5},{5,4},{6,7},{7,6},{8,9},{9,8},{10,11... | collective-permute-start | bytes 294920 | tf_op jit(solution)/shard_map/ppermute | solution.py:318
  106.5 9.8 %collective-permute-start.30 = (bf16[24,1792]{1,0:T(8,128)(2,1)S(1)}, bf16[24,1792]{1,0:T(8,128)(2,1)S(1)}, u32[]{:S(2)}, u32[]{:S(2)}) collective-permute-start(bf16[24,1792]{1,0:T(8,128)(2,1)S(1)} %get-tuple-element.88), channel_id=1, source_target_pairs={{0,4},{4,0},{8,12},{12,8},{1,5},{5,1},{9,13},{13,9},{2,6},{6,2},{1... | collective-permute-start | bytes 258056 | tf_op jit(solution)/shard_map/ppermute | solution.py:326
  109.5 10.0 %collective-permute-start.31 = (bf16[24,1792]{1,0:T(8,128)(2,1)S(1)}, bf16[24,1792]{1,0:T(8,128)(2,1)S(1)}, u32[]{:S(2)}, u32[]{:S(2)}) collective-permute-start(bf16[24,1792]{1,0:T(8,128)(2,1)S(1)} %get-tuple-element.89), channel_id=1, source_target_pairs={{0,8},{4,12},{8,0},{12,4},{1,9},{5,13},{9,1},{13,5},{2,10},{6,14},... | collective-permute-start | bytes 258056 | tf_op jit(solution)/shard_map/ppermute | solution.py:326
  110.3 9.2 %collective-permute-start.32 = (bf16[24,1792]{1,0:T(8,128)(2,1)S(1)}, bf16[24,1792]{1,0:T(8,128)(2,1)S(1)}, u32[]{:S(2)}, u32[]{:S(2)}) collective-permute-start(bf16[24,1792]{1,0:T(8,128)(2,1)S(1)} %get-tuple-element.90), channel_id=1, source_target_pairs={{0,12},{4,8},{8,4},{12,0},{1,13},{5,9},{9,5},{13,1},{2,14},{6,10},... | collective-permute-start | bytes 258056 | tf_op jit(solution)/shard_map/ppermute | solution.py:326
  114.6 12.3 %collective-permute-start.25 = (bf16[24,1792]{1,0:T(8,128)(2,1)S(1)}, bf16[24,1792]{1,0:T(8,128)(2,1)S(1)}, u32[]{:S(2)}, u32[]{:S(2)}) collective-permute-start(bf16[24,1792]{1,0:T(8,128)(2,1)S(1)} %get-tuple-element.83), channel_id=1, source_target_pairs={{0,8},{4,12},{8,0},{12,4},{1,9},{5,13},{9,1},{13,5},{2,10},{6,14},... | collective-permute-start | bytes 258056 | tf_op jit(solution)/shard_map/ppermute | solution.py:326
  116.3 10.5 %collective-permute-start.26 = (bf16[24,1792]{1,0:T(8,128)(2,1)S(1)}, bf16[24,1792]{1,0:T(8,128)(2,1)S(1)}, u32[]{:S(2)}, u32[]{:S(2)}) collective-permute-start(bf16[24,1792]{1,0:T(8,128)(2,1)S(1)} %get-tuple-element.84), channel_id=1, source_target_pairs={{0,12},{4,8},{8,4},{12,0},{1,13},{5,9},{9,5},{13,1},{2,14},{6,10},... | collective-permute-start | bytes 258056 | tf_op jit(solution)/shard_map/ppermute | solution.py:326
  (11 other events, 70.7 us)
